TPU v7x, 128 devices: a whole 4x4x4 slice. The times are simulated.
128 devices in a mesh: ctx: 32 (over z, x, y_hi), head: 4 (over y_lo, core).
Axes of the slice: x: 4, y: 4 (y_hi: 2, y_lo: 2; y = y_hi * 2 + y_lo), z: 4, core: 2. Of those that a mesh axis runs over, the one named last changes fastest.
Arguments:
- probe_vectors: bfloat16 [1024, 8192], P('ctx', 'head'), may hold values from -160 to 160
- lookup_tensor: bfloat16 [32768, 1024], P('ctx', 'head'), may hold values from -4.5 to 4.5
- payload_tensor: bfloat16 [32768, 1024], P('ctx', 'head'), may hold values from -6 to 6
- sequence_locations: int32 [1024], replicated, may hold values from 0 to 32767, as said below
- attention_return_matrix: bfloat16 [8192, 8192], P('head', 'ctx'), may hold values from -0.0625 to 0.0625
- skip_stream_state: bfloat16 [1024, 8192], P('head', 'ctx'), may hold values from -4 to 4
- early_rescaling_factor: float32 [8192], P('ctx'), may hold values from 0.5 to 1.5
- lexicon_projection_matrix: bfloat16 [8192, 65536], P(None, ('ctx', 'head')), may hold values from -0.1875 to 0.1875
- calibrating_divisor: float32 [1024], replicated, may hold values from 0.02 to 1
- desired_tokens_list: int32 [1024], replicated, may hold values from 0 to 65535
Outputs:
- hidden: bfloat16 [1024, 8192], P('head', 'ctx')
- logprob: float32 [1024], replicated
Inputs may be any that keep to these rules, and one draw needn't show every extreme that they name: `sequence_locations`: query i stands at a position from i * 32 to (i + 1) * 32 - 1; the last query stands at 32767.
All inputs are finite; a program needn't handle non-finite values.
Results may differ from a plain program's by a relative error of at most 0.0014.
The roundings to bfloat16 on the way count: a program that leaves them out, or rounds other values in their place, can miss the bound.
Values may be sent and summed in bfloat16 or wider, within the bound.
A program may use at most 192 MiB of HBM per device.

v0:
```python
import math

import jax
import jax.numpy as jnp
from jax import lax
from jax.sharding import Mesh
from jax.sharding import PartitionSpec as P

D = 8192
QUERY_HEAD_COUNT = 64
KEY_VALUE_HEADS = 8
HEAD_SIZE = 128
CTX = ("ctx_0", "ctx_1", "ctx_2")
HEAD = ("head_0", "head_1")
CTX_HEAD = ("ctx_0", "ctx_1", "ctx_2", "head_0", "head_1")


neg_big = -1e30
eps = 1e-05


def copy_for_each(x, axis):
    devices = lax.axis_size(axis)
    return lax.all_to_all(jnp.broadcast_to(x[None], (devices, *x.shape)), axis, 0, 0, tiled=True)


def taken_together(x, axis):
    everything = copy_for_each(x, axis)
    return jnp.max(everything, axis=0)


def sent_together(arrays, axis, dim, along):
    widths = [math.prod(a.shape[along:]) for a in arrays]
    both = jnp.concatenate(
        [a.reshape(*a.shape[:along], w) for a, w in zip(arrays, widths)], axis=along
    )
    result = lax.psum_scatter(both, axis, scatter_dimension=dim, tiled=True)
    tiles = jnp.split(result, [sum(widths[:k]) for k in range(1, len(widths))], axis=along)
    return tuple(
        (b.reshape(*result.shape[:along], *a.shape[along:]) for a, b in zip(arrays, tiles))
    )


def in_blocks(x, dim, devices):
    shape = x.shape
    tiles = x.reshape(*shape[:dim], devices, shape[dim] // devices, *shape[dim + 1 :])
    return jnp.moveaxis(tiles, dim, 0)


def sent_and_summed(x, axis, dim):
    devices = lax.axis_size(axis)
    tiles = lax.all_to_all(in_blocks(x, dim, devices), axis, 0, 0, tiled=True)
    return jnp.sum(tiles, axis=0)


def of_everyone(x, axis):
    everything = copy_for_each(x, axis)
    return jnp.sum(everything, axis=0)


def collected_together(x, axis):
    leaves = jax.tree.leaves(x)
    sequence = sorted(range(len(leaves)), key=lambda k: -leaves[k].size)
    width = (1, *leaves[sequence[0]].shape)[-1]
    lines = [
        jnp.pad(leaves[k].reshape(-1), (0, -leaves[k].size % width)).reshape(-1, width)
        for k in sequence
    ]
    both, at, found = (lax.all_gather(jnp.concatenate(lines), axis), 0, {})
    for k, line in zip(sequence, lines):
        slab = both[:, at : at + len(line)].reshape(len(both), -1)
        found[k] = slab[:, : leaves[k].size].reshape(-1, *leaves[k].shape)
        at += len(line)
    numbers = iter(range(len(leaves)))
    return jax.tree.map(lambda _: found[next(numbers)], x)


def joined_all(x, axes, combine):
    for axis in axes:
        pieces = collected_together(x, axis)
        x = jax.tree.map(lambda part: part[0], pieces)
        for k in range(1, lax.axis_size(axis)):
            x = combine(x, jax.tree.map(lambda part: part[k], pieces))
    return x


def unite_vocab(first, second):
    peak_first, total_first, picked_first = first
    peak_second, total_second, picked_second = second
    joined = jnp.maximum(peak_first, peak_second)
    total = total_first * jnp.exp(peak_first - joined) + total_second * jnp.exp(
        peak_second - joined
    )
    return (joined, total, picked_first + picked_second)


def local_attention(every_query, lookup_tensor, payload_tensor, sequence_locations, key_start):
    total_rows = every_query.shape[0]
    ctx_len = lookup_tensor.shape[0]
    kv_here = lookup_tensor.shape[1] // HEAD_SIZE
    group_size = QUERY_HEAD_COUNT // KEY_VALUE_HEADS
    scale_factor = HEAD_SIZE ** (-0.5)
    row_block = min(512, total_rows)
    query_heads = every_query.reshape(total_rows, kv_here, group_size, HEAD_SIZE)
    key_heads = lookup_tensor.reshape(ctx_len, kv_here, HEAD_SIZE)
    value_heads = payload_tensor.reshape(ctx_len, kv_here, HEAD_SIZE)
    key_pos = key_start + jnp.arange(ctx_len, dtype=jnp.int32)
    maxima, sums, accums = ([], [], [])
    for row_start in range(0, total_rows, row_block):
        row_pos = sequence_locations[row_start : row_start + row_block]
        visible = key_pos[None, None, :] <= row_pos[:, None, None]
        head_max, head_sum, head_acc = ([], [], [])
        for kv_head in range(kv_here):
            scores = (
                jnp.einsum(
                    "qhd,kd->qhk",
                    query_heads[row_start : row_start + row_block, kv_head],
                    key_heads[:, kv_head],
                    preferred_element_type=jnp.float32,
                )
                * scale_factor
            )
            block_max = jnp.max(jnp.where(visible, scores, neg_big), axis=-1)
            weights = jnp.where(visible, jnp.exp(scores - block_max[..., None]), 0.0)
            head_sum.append(jnp.sum(weights, axis=-1))
            head_max.append(block_max)
            head_acc.append(
                jnp.einsum(
                    "qhk,kd->qhd",
                    weights.astype(jnp.bfloat16),
                    value_heads[:, kv_head],
                    preferred_element_type=jnp.float32,
                )
            )
        maxima.append(jnp.concatenate(head_max, axis=1))
        sums.append(jnp.concatenate(head_sum, axis=1))
        accums.append(jnp.concatenate(head_acc, axis=1))
    return (
        jnp.concatenate(maxima, axis=0),
        jnp.concatenate(sums, axis=0),
        jnp.concatenate(accums, axis=0),
    )


def shards(
    probe_vectors,
    lookup_tensor,
    payload_tensor,
    sequence_locations,
    attention_return_matrix,
    skip_stream_state,
    early_rescaling_factor,
    lexicon_projection_matrix,
    calibrating_divisor,
    desired_tokens_list,
):
    heads_here = probe_vectors.shape[1] // HEAD_SIZE
    every_query = lax.all_gather(probe_vectors, CTX, axis=0, tiled=True)
    key_start = lax.axis_index(CTX) * lookup_tensor.shape[0]
    local_max, local_sum, local_acc = local_attention(
        every_query, lookup_tensor, payload_tensor, sequence_locations, key_start
    )
    global_max = taken_together(local_max.astype(jnp.bfloat16), CTX).astype(local_max.dtype)
    rescale = jnp.exp(local_max - global_max)
    acc_rows, sum_rows = sent_together(
        (local_acc * rescale[..., None], local_sum * rescale), CTX, 0, 2
    )
    attn = (
        (acc_rows / sum_rows[..., None])
        .astype(jnp.bfloat16)
        .reshape(acc_rows.shape[0], heads_here * HEAD_SIZE)
    )
    mixed_part = jnp.dot(
        lax.all_gather(attn, CTX, axis=0, tiled=True),
        attention_return_matrix,
        preferred_element_type=jnp.float32,
    )
    mixed_rows = sent_and_summed(mixed_part, HEAD, 0)
    hidden = (skip_stream_state.astype(jnp.float32) + mixed_rows).astype(jnp.bfloat16)
    widened = hidden.astype(jnp.float32)
    square_total = of_everyone(jnp.sum(widened * widened, axis=1), CTX)
    normed = (
        widened * lax.rsqrt(square_total / D + eps)[:, None] * early_rescaling_factor[None, :]
    ).astype(jnp.bfloat16)
    full_rows = lax.all_gather(normed, CTX, axis=1, tiled=True)
    early_class_energies = jnp.dot(
        lax.all_gather(full_rows, HEAD, axis=0, tiled=True),
        lexicon_projection_matrix,
        preferred_element_type=jnp.float32,
    )
    tempered_affinities = early_class_energies / calibrating_divisor[:, None]
    vocab_here = lexicon_projection_matrix.shape[1]
    offset = (lax.axis_index(CTX) * lax.axis_size(HEAD) + lax.axis_index(HEAD)) * vocab_here
    column_ids = jnp.arange(vocab_here, dtype=jnp.int32)[None, :] + offset
    picked = jnp.sum(
        jnp.where(column_ids == desired_tokens_list[:, None], tempered_affinities, 0.0), axis=1
    )
    local_peak = jnp.max(tempered_affinities, axis=1)
    local_total = jnp.sum(jnp.exp(tempered_affinities - local_peak[:, None]), axis=1)
    peak, total, target_logit = joined_all((local_peak, local_total, picked), CTX_HEAD, unite_vocab)
    logprob = target_logit - peak - jnp.log(total)
    return (hidden, logprob)


def solution(mesh):
    torus = Mesh(
        mesh.devices.reshape(4, 4, 2, 2, 2), ("ctx_0", "ctx_1", "ctx_2", "head_0", "head_1")
    )
    placed = (
        P(CTX, HEAD),
        P(CTX, HEAD),
        P(CTX, HEAD),
        P(),
        P(HEAD, CTX),
        P(HEAD, CTX),
        P(CTX),
        P(None, CTX_HEAD),
        P(),
        P(),
    )
    return jax.shard_map(
        shards, mesh=torus, in_specs=placed, out_specs=(P(HEAD, CTX), P()), check_vma=False
    )
```

profile of v0, /device:TPU:1, one launch (start us, length us, event | category | flops | bytes accessed | tf_op | source)
XLA Modules:
  0.0 1000.2 jit_solution(12280744665633798866)
XLA Ops:
  7.2 0.0 copy-start
  7.2 0.0 all-gather.15.cloned.1.call-start
  7.2 0.7 all-gather.15.cloned.1.call-update
  7.9 1.2 copy.117
  9.2 1.2 copy.119
  10.5 0.8 fusion.82
  11.2 0.7 broadcast_compare_fusion.1
  11.9 82.4 %all-gather.15.cloned.1.call-done = bf16[1024,2048]{1,0:T(8,128)(2,1)} async-done(((bf16[32,2048]{1,0:T(8,128)(2,1)}), bf16[1024,2048]{1,0:T(8,128)(2,1)}) %all-gather.15.cloned.1.call-update) | async-done | bytes 4194320 | tf_op jit(solution)/shard_map/all_gather | solution.py:158
  94.2 6.4 copy.115
  100.6 8.8 select_reduce_fusion.3
  109.4 0.0 copy-done.3
  109.4 15.3 %fusion = (f32[512,8]{0,1:T(8,128)S(1)}, f32[512,8]{0,1:T(8,128)S(1)}, f32[512,8,1024]{2,0,1:T(8,128)}) fusion(f32[512,8,1024]{2,0,1:T(8,128)} %get-tuple-element.31, f32[512,8]{0,1:T(8,128)S(1)} %get-tuple-element.30, pred[512,1024]{1,0:T(8,128)(4,1)S(1)} %get-tuple-element.23, bf16[1024,2,128]{0,2,1:T(8,128)(2,1)S(1)} %bitcast.321, ...), kind=kOutput, calls=%fused_computation.9 | convolution fusion | flops 1103093760 | bytes 35438592 | tf_op jit(solution)/shard_map/qhd,kd->qhk/dot_general | solution.py:115
  124.7 8.5 fusion.14
  133.1 7.4 select_reduce_fusion.1
  140.6 8.5 fusion.10
  149.0 15.3 %fusion.4 = (f32[512,8]{0,1:T(8,128)S(1)}, f32[512,8]{0,1:T(8,128)S(1)}, f32[512,8,1024]{2,0,1:T(8,128)}) fusion(f32[512,8,1024]{2,0,1:T(8,128)} %get-tuple-element.28, f32[512,8]{0,1:T(8,128)S(1)} %get-tuple-element.27, pred[512,1024]{1,0:T(8,128)(4,1)S(1)} %get-tuple-element.24, bf16[1024,2,128]{0,2,1:T(8,128)(2,1)S(1)} %bitcast.323, ...), kind=kOutput, calls=%fused_computation.13 | convolution fusion | flops 1103093760 | bytes 35438592 | tf_op jit(solution)/shard_map/qhd,kd->qhk/dot_general | solution.py:115
  164.3 8.8 fusion.12
  173.1 2.5 copy-done.2
  175.6 11.1 %fusion.2 = (f32[512,8]{0,1:T(8,128)S(1)}, f32[512,8]{0,1:T(8,128)S(1)}) fusion(f32[512,8,1024]{2,0,1:T(8,128)} %get-tuple-element.32, f32[512,8]{0,1:T(8,128)S(1)} %get-tuple-element.5, pred[512,1024]{1,0:T(8,128)(4,1)S(1)} %get-tuple-element.23, f32[512,8]{0,1:T(8,128)S(1)} %get-tuple-element.7, f32[512,8,1024]{2,0,1:T(8,128)S(1)} %copy-done.2, ...), kind=kLoop, calls=%fused_computation.11 | loop fusion | flops 33546240 | bytes 34668544 | tf_op jit(solution)/shard_map/reduce_sum | solution.py:125
  186.7 1.1 broadcast_in_dim.79
  187.8 5.3 all-to-all-start
  193.1 0.0 reduce-scatter.2.cloned.1.call-start
  193.1 8.5 fusion.8
  201.6 9.5 all-to-all-done
  211.1 0.2 reduce_max.58
  211.3 4.7 copy.126
  216.0 6.4 maximum_multiply_fusion
  222.5 0.0 copy-done.1
  222.5 6.1 pad_maximum_fusion
  228.5 0.0 reduce-scatter.2.cloned.1.call-update
  228.6 0.0 all-gather.17.cloned.1.call-start
  228.6 357.1 %reduce-scatter.2.cloned.1.call-done = f32[32,16,129]{2,0,1:T(8,128)} async-done(((f32[1024,16,129]{2,0,1:T(8,128)}), f32[32,16,129]{2,0,1:T(8,128)}) %reduce-scatter.2.cloned.1.call-update) | async-done | bytes 264208 | tf_op jit(solution)/shard_map/reduce_scatter | solution.py:37
  585.7 1.1 slice_reduce_fusion
  586.8 1.7 copy_bitcast_fusion
  588.6 0.0 all-gather.17.cloned.1.call-update
  588.6 0.0 all-gather.19.cloned.1.call-start
  588.7 84.5 %all-gather.17.cloned.1.call-done = bf16[1024,2048]{1,0:T(8,128)(2,1)} async-done(((bf16[32,2048]{1,0:T(8,128)(2,1)}), bf16[1024,2048]{1,0:T(8,128)(2,1)}) %all-gather.17.cloned.1.call-update) | async-done | bytes 4194320 | tf_op jit(solution)/shard_map/all_gather | solution.py:174
  673.2 0.0 copy-done
  673.2 3.4 fusion.84
  676.6 16.9 %all_to_all.16 = f32[4,256,256]{2,1,0:T(8,128)S(1)} all-to-all(f32[4,256,256]{2,1,0:T(8,128)S(1)} %bitcast.315), channel_id=1, replica_groups=mesh['ctx_0'=4,'ctx_1'=4,'ctx_2'=2,'head_0'=2,'head_1'=2] {'head_0','hea..., dimensions={0} | all-to-all | bytes 2097152 | tf_op jit(solution)/shard_map/all_to_all | solution.py:52
  693.5 0.1 reduce_sum.85
  693.6 0.0 copy-done.5
  693.6 0.1 fusion.24
  693.7 0.0 copy-start.4
  693.8 14.4 %all_to_all.17 = f32[32,1,256]{2,1,0:T(1,128)S(1)} all-to-all(f32[32,1,256]{2,1,0:T(1,128)S(1)} %broadcast_in_dim.80), channel_id=1, replica_groups=mesh['ctx_0'=4,'ctx_1'=4,'ctx_2'=2,'head_0'=2,'head_1'=2] {'ctx_0','ctx_..., dimensions={0} | all-to-all | bytes 65536 | tf_op jit(solution)/shard_map/all_to_all | solution.py:24
  708.2 0.1 reduce_sum.87
  708.2 0.0 copy-done.7
  708.2 0.7 fusion.26
  709.0 0.0 all-gather.19.cloned.1.call-update
  709.0 0.0 all-gather.21.cloned.1.call-start
  709.0 77.2 %all-gather.19.cloned.1.call-done = bf16[256,8192]{1,0:T(8,128)(2,1)} async-done(((bf16[256,256]{1,0:T(8,128)(2,1)}), bf16[256,8192]{1,0:T(8,128)(2,1)}) %all-gather.19.cloned.1.call-update) | async-done | bytes 4194320 | tf_op jit(solution)/shard_map/all_gather | solution.py:185
  786.2 0.0 all-gather.21.cloned.1.call-update
  786.3 0.0 copy-start.6
  786.3 153.9 %all-gather.21.cloned.1.call-done = bf16[1024,8192]{1,0:T(8,128)(2,1)} async-done(((bf16[256,8192]{1,0:T(8,128)(2,1)}), bf16[1024,8192]{1,0:T(8,128)(2,1)}) %all-gather.21.cloned.1.call-update) | async-done | bytes 16777232 | tf_op jit(solution)/shard_map/all_gather | solution.py:187
  940.2 17.1 %fusion.83 = (f32[1024]{0:T(1024)S(1)}, f32[1024,512]{0,1:T(8,128)S(1)}) fusion(f32[1024]{0:T(1024)S(1)} %copy-done.8, bf16[1024,8192]{1,0:T(8,128)(2,1)} %all-gather.21.cloned.1.call-done, bf16[8192,512]{1,0:T(8,128)(2,1)} %param.17), kind=kOutput, calls=%fused_computation.154 | convolution fusion | flops 8590982144 | bytes 27271168 | tf_op jit(solution)/shard_map/dot_general | solution.py:186
  957.3 0.5 exponential_reduce_fusion
  957.8 9.7 all-gather.5
  967.5 0.1 fusion.54
  967.6 9.3 all-gather.6
  976.9 0.1 fusion.44
  977.0 4.8 all-gather.7
  981.8 3.3 all-gather.8
  985.1 7.9 all-gather.9
  993.1 0.6 log_subtract_fusion
  (31 shorter events, 0.3 us)
Async XLA Ops:
  7.2 666.0 %copy-start = (bf16[2048,256]{1,0:T(8,128)(2,1)S(1)}, bf16[2048,256]{1,0:T(8,128)(2,1)}, u32[]{:S(2)}) copy-start(bf16[2048,256]{1,0:T(8,128)(2,1)} %param.14) | copy-start | bytes 3145732
  7.2 87.1 %all-gather.15.cloned.1.call-start = ((), (), s32[]{:S(2)}) async-start(), calls=%async_computation.4 | async-start | bytes 4325376 | tf_op jit(solution)/shard_map/all_gather | solution.py:158
  100.6 8.8 copy-start.3
  164.3 11.3 %copy-start.2 = (f32[512,8,1024]{2,0,1:T(8,128)S(1)}, f32[512,8,1024]{2,0,1:T(8,128)}, u32[]{:S(2)}) copy-start(f32[512,8,1024]{2,0,1:T(8,128)} %get-tuple-element.29) | copy-start | bytes 50331652
  187.8 23.3 %all-to-all-start = ((bf16[32,1024,16]{1,2,0:T(8,128)(2,1)}), bf16[32,1024,16]{1,2,0:T(8,128)(2,1)S(1)}, u32[]{:S(2)}, u32[]{:S(2)}) async-start(bf16[32,1024,16]{1,2,0:T(8,128)(2,1)} %broadcast_in_dim.79), calls=%async_computation | async-start | bytes 2097152 | tf_op jit(solution)/shard_map/all_to_all | solution.py:24
  193.1 392.7 %reduce-scatter.2.cloned.1.call-start = ((), (), s32[]{:S(2)}) async-start(), calls=%async_computation.5 | async-start | bytes 17301504 | tf_op jit(solution)/shard_map/reduce_scatter | solution.py:37
  216.0 6.4 copy-start.1
  228.5 465.1 %copy-start.5 = (bf16[256,256]{1,0:T(8,128)(2,1)S(1)}, bf16[256,256]{1,0:T(8,128)(2,1)}, u32[]{:S(2)}) copy-start(bf16[256,256]{1,0:T(8,128)(2,1)} %param.15) | copy-start | bytes 393220
  228.5 479.7 %copy-start.7 = (f32[256]{0:T(256)S(1)}, f32[256]{0:T(256)}, u32[]{:S(2)}) copy-start(f32[256]{0:T(256)} %param.16) | copy-start | bytes 3076
  228.5 711.7 %copy-start.8 = (f32[1024]{0:T(1024)S(1)}, f32[1024]{0:T(1024)}, u32[]{:S(2)}) copy-start(f32[1024]{0:T(1024)} %param.18) | copy-start | bytes 12292
  228.6 444.6 %all-gather.17.cloned.1.call-start = ((), (), s32[]{:S(2)}) async-start(), calls=%async_computation.6 | async-start | bytes 4325376 | tf_op jit(solution)/shard_map/all_gather | solution.py:174
  588.6 197.6 %all-gather.19.cloned.1.call-start = ((), (), s32[]{:S(2)}) async-start(), calls=%async_computation.7 | async-start | bytes 4325376 | tf_op jit(solution)/shard_map/all_gather | solution.py:185
  693.7 263.5 %copy-start.4 = (bf16[256,256]{1,0:T(8,128)(2,1)}, bf16[256,256]{1,0:T(8,128)(2,1)S(1)}, u32[]{:S(2)}) copy-start(bf16[256,256]{1,0:T(8,128)(2,1)S(1)} %get-tuple-element.17) | copy-start | bytes 393220
  709.0 231.2 %all-gather.21.cloned.1.call-start = ((), (), s32[]{:S(2)}) async-start(), calls=%async_computation.8 | async-start | bytes 20971520 | tf_op jit(solution)/shard_map/all_gather | solution.py:187
  786.3 171.0 %copy-start.6 = (s32[1024]{0:T(1024)S(1)}, s32[1024]{0:T(1024)}, u32[]{:S(2)}) copy-start(s32[1024]{0:T(1024)} %param.19) | copy-start | bytes 12292
Sparse Core Ops, SparseCore 0:
  11.1 83.0 all-gather.14
  228.7 357.0 reduce-scatter.1
  589.4 83.7 all-gather.16
  709.1 77.0 all-gather.18
  787.7 152.3 all-gather.20
where the time goes:
time: 1000 us
  waiting for transfers between devices  765 us (76%)
  matrix products  101 us (10%)
  blocking collectives  66.2 us (7%)
  other arithmetic  28.6 us (3%)
  local copies, waits for them, and re-layouts  19.1 us (2%)
  between operations  14.1 us (1%)
    reduce_scatter x1, waiting for transfers between devices, sent_together(): result = lax.psum_scatter(both, axis, scatter_dimension=dim, tiled=True)  357 us
    all_gather x1, waiting for transfers between devices, shards(): lax.all_gather(full_rows, HEAD, axis=0, tiled=True)  154 us
    all_gather x1, waiting for transfers between devices, shards(): lax.all_gather(attn, CTX, axis=0, tiled=True)  84.5 us
    all_gather x1, waiting for transfers between devices, shards(): every_query = lax.all_gather(probe_vectors, CTX, axis=0, tiled=True)  82.4 us
    all_gather x1, waiting for transfers between devices, shards(): full_rows = lax.all_gather(normed, CTX, axis=1, tiled=True)  77.2 us
    dot_general x4, matrix products, local_attention(): jnp.einsum('qhd,kd->qhk', query_heads[row_start:row_start + row_block, kv...  46.7 us
    all_gather x5, blocking collectives, collected_together(): both, at, found = (lax.all_gather(jnp.concatenate(lines), axis), 0, {})  34.9 us
    dot_general x4, matrix products, local_attention(): jnp.einsum('qhk,kd->qhd', weights.astype(jnp.bfloat16), value_heads[:, kv...  34.2 us
  transfers between devices with their start and end apart: 6, of which 6 were waited for; matrix products, arithmetic and copies ran while one was open for 1% of the time, Pallas kernels for 0%

commit v1 on v0

v1 whole, which is shorter than its diff:
```python
import jax
import jax.numpy as jnp
from jax import lax
from jax.experimental import pallas as pl
from jax.experimental.pallas import tpu as pltpu
from jax.sharding import Mesh
from jax.sharding import PartitionSpec as P

D = 8192
EPS = 1e-05
LOW = -1e30
LOG2E = 1.4426950408889634
EXP2_SCALE = 128 ** (-0.5) * LOG2E
CTX = ("ctx_0", "ctx_1", "ctx_2")
HEAD = ("head_0", "head_1")
CTX_HEAD = CTX + HEAD
F32 = jnp.float32
BF16 = jnp.bfloat16
MESH = pl.DeviceIdType.MESH


def at_z(p):
    return {"ctx_0": p}


def at_x(p):
    return {"ctx_1": p}


def at_y(p):
    return {"ctx_2": lax.div(p, 2), "head_0": lax.rem(p, 2)}


def at_core(p):
    return {"head_1": p}


def around(p, d):
    return lax.rem(p + d, 4)


def remote(src, dst, ssem, rsem, dev):
    return pltpu.make_async_remote_copy(
        src_ref=src, dst_ref=dst, send_sem=ssem, recv_sem=rsem, device_id=dev, device_id_type=MESH
    )


def greet(dev):
    pl.semaphore_signal(pltpu.get_barrier_semaphore(), inc=1, device_id=dev, device_id_type=MESH)


def attend_kernel(
    q_hbm, k_hbm, v_hbm, loc_ref, out_ref,
    qbuf, kbuf, vbuf, m_s, l_s, acc, stat, racc, rstat,
    q_ss, q_rs, kv_ls, kv_ss, kv_rs, o_ss, o_rs,
):
    z, x, yh = lax.axis_index("ctx_0"), lax.axis_index("ctx_1"), lax.axis_index("ctx_2")
    k_me = 2 * x + yh
    plus, minus, opp = around(z, 1), around(z, 3), around(z, 2)
    diagonal = x == z

    greet(at_z(plus))
    greet(at_z(minus))
    for i in range(8):
        @pl.when(i != k_me)
        def _():
            greet({"ctx_1": i // 2, "ctx_2": i % 2})
    for i in range(8):
        src_z, src_y = i // 2, i % 2
        @pl.when(jnp.logical_not(diagonal & (src_z == z) & (src_y == yh)))
        def _():
            greet({"ctx_0": src_z, "ctx_1": z, "ctx_2": src_y})
    pl.semaphore_wait(pltpu.get_barrier_semaphore(), 2 + 7 + jnp.where(diagonal, 7, 8))

    slot_me = 2 * z + yh
    for i in range(8):
        to_self = diagonal & (i == k_me)
        @pl.when(jnp.logical_not(to_self))
        def _():
            remote(q_hbm, qbuf.at[slot_me], q_ss.at[i], q_rs.at[slot_me],
                   {"ctx_0": x, "ctx_1": i // 2, "ctx_2": i % 2}).start()
        @pl.when(to_self)
        def _():
            pltpu.make_async_copy(q_hbm, qbuf.at[slot_me], q_rs.at[slot_me]).start()

    own_k = pltpu.make_async_copy(k_hbm, kbuf.at[z], kv_ls.at[0])
    own_v = pltpu.make_async_copy(v_hbm, vbuf.at[z], kv_ls.at[1])
    own_k.start()
    own_v.start()
    k_plus = remote(k_hbm, kbuf.at[z], kv_ss.at[0], kv_rs.at[0], at_z(plus))
    v_minus = remote(v_hbm, vbuf.at[z], kv_ss.at[1], kv_rs.at[1], at_z(minus))
    v_plus = remote(v_hbm, vbuf.at[z], kv_ss.at[2], kv_rs.at[2], at_z(plus))
    k_minus = remote(k_hbm, kbuf.at[z], kv_ss.at[3], kv_rs.at[3], at_z(minus))
    k_plus.start()
    v_minus.start()
    v_plus.start()
    k_minus.start()
    k_on = remote(kbuf.at[minus], kbuf.at[minus], kv_ss.at[4], kv_rs.at[4], at_z(plus))
    v_on = remote(vbuf.at[plus], vbuf.at[plus], kv_ss.at[5], kv_rs.at[5], at_z(minus))

    m_s[...] = jnp.full(m_s.shape, LOW, F32)
    l_s[...] = jnp.zeros(l_s.shape, F32)
    acc[...] = jnp.zeros(acc.shape, F32)

    own_k.wait()
    own_v.wait()
    for i in range(8):
        remote(qbuf.at[i], qbuf.at[i], q_ss.at[0], q_rs.at[i], at_z(plus)).wait_recv()

    def tile(s, zo, g, masked):
        q = jnp.concatenate(
            [qbuf[s, :, (g * 8 + j) * 128 : (g * 8 + j + 1) * 128] for j in range(8)], axis=0
        )
        raw = lax.dot_general(
            q, kbuf[zo, :, g * 128 : (g + 1) * 128], (((1,), (1,)), ((), ())),
            preferred_element_type=F32,
        )
        if masked:
            base = 8 * zo + k_me
            first = pl.multiple_of(base * 32, 32)
            loc = loc_ref[pl.ds(first, 32), :] - base * 1024
            loc = jnp.concatenate([loc] * 8, axis=0)
            pos = lax.broadcasted_iota(jnp.int32, raw.shape, 1)
            raw = jnp.where(pos <= loc, raw, LOW)
        top = jnp.max(raw, axis=1, keepdims=True)
        w = jnp.exp2((raw - top) * EXP2_SCALE)
        total = jnp.sum(w, axis=1, keepdims=True)
        part = jnp.dot(
            w.astype(BF16), vbuf[zo, :, g * 128 : (g + 1) * 128], preferred_element_type=F32
        )
        m_old = m_s[s, g]
        m_new = jnp.maximum(m_old, top)
        a = jnp.exp2((m_old - m_new) * EXP2_SCALE)
        b = jnp.exp2((top - m_new) * EXP2_SCALE)
        m_s[s, g] = m_new
        l_s[s, g] = l_s[s, g] * a + total * b
        acc[s, g] = acc[s, g] * a + part * b

    def work(s, zo):
        chunk = 8 * lax.div(s, 2) + 2 * z + lax.rem(s, 2)
        block = 8 * zo + k_me

        @pl.when(chunk > block)
        def _():
            for g in range(2):
                tile(s, zo, g, False)

        @pl.when(chunk == block)
        def _():
            for g in range(2):
                tile(s, zo, g, True)

    def acc_copy(s):
        return remote(acc.at[s], racc.at[k_me], o_ss.at[0, s], o_rs.at[0, k_me],
                      {"ctx_1": lax.div(s, 2), "ctx_2": lax.rem(s, 2)})

    def stat_copy(s):
        return remote(stat.at[s], rstat.at[k_me], o_ss.at[1, s], o_rs.at[1, k_me],
                      {"ctx_1": lax.div(s, 2), "ctx_2": lax.rem(s, 2)})

    @pl.loop(0, 4)
    def _(p):
        @pl.when(p == 1)
        def _():
            k_plus.wait_recv()
            k_on.start()
            v_minus.wait_recv()
            v_on.start()
            v_plus.wait_recv()

        @pl.when(p == 2)
        def _():
            k_minus.wait_recv()

        @pl.when(p == 3)
        def _():
            k_on.wait_recv()
            v_on.wait_recv()

        zo = around(z, jnp.where(p == 1, 3, jnp.where(p == 2, 1, jnp.where(p == 3, 2, 0))))

        @pl.loop(0, 8)
        def _(i):
            s = lax.rem(i + 1 + k_me, 8)
            work(s, zo)

            @pl.when(p == 3)
            def _():
                lane = lax.broadcasted_iota(jnp.int32, (32, 128), 1)
                ms = jnp.full((32, 128), LOW, F32)
                ls = jnp.zeros((32, 128), F32)
                for h in range(16):
                    rows = slice((h % 8) * 32, (h % 8) * 32 + 32)
                    ms = jnp.where(lane == h, m_s[s, h // 8, rows, :], ms)
                    ls = jnp.where(lane == h, l_s[s, h // 8, rows, :], ls)
                stat[s, 0] = ms
                stat[s, 1] = ls

                @pl.when(s != k_me)
                def _():
                    acc_copy(s).start()
                    stat_copy(s).start()

                @pl.when(s == k_me)
                def _():
                    pltpu.make_async_copy(acc.at[s], racc.at[k_me], o_rs.at[0, k_me]).start()
                    pltpu.make_async_copy(stat.at[s], rstat.at[k_me], o_rs.at[1, k_me]).start()

    for i in range(8):
        remote(stat.at[i], rstat.at[i], o_ss.at[1, i], o_rs.at[1, i], at_z(plus)).wait_recv()
        remote(acc.at[i], racc.at[i], o_ss.at[0, i], o_rs.at[0, i], at_z(plus)).wait_recv()

    top = rstat[0, 0]
    for i in range(1, 8):
        top = jnp.maximum(top, rstat[i, 0])
    shares = [jnp.exp2((rstat[i, 0] - top) * EXP2_SCALE) for i in range(8)]
    den = shares[0] * rstat[0, 1]
    for i in range(1, 8):
        den = den + shares[i] * rstat[i, 1]
    for h in range(16):
        rows = slice((h % 8) * 32, (h % 8) * 32 + 32)
        num = shares[0][:, h : h + 1] * racc[0, h // 8, rows, :]
        for i in range(1, 8):
            num = num + shares[i][:, h : h + 1] * racc[i, h // 8, rows, :]
        out_ref[:, h * 128 : (h + 1) * 128] = (num / den[:, h : h + 1]).astype(BF16)

    for i in range(8):
        @pl.when(jnp.logical_not(diagonal & (i == k_me)))
        def _():
            remote(q_hbm, qbuf.at[i], q_ss.at[i], q_rs.at[i], at_z(plus)).wait_send()
        @pl.when(i != k_me)
        def _():
            acc_copy(i).wait_send()
            stat_copy(i).wait_send()
    for c in (k_plus, v_minus, v_plus, k_minus, k_on, v_on):
        c.wait_send()


def attend(q, k, v, loc):
    return pl.pallas_call(
        attend_kernel,
        out_shape=jax.ShapeDtypeStruct((32, 2048), BF16),
        in_specs=[pl.BlockSpec(memory_space=pl.ANY)] * 3 + [pl.BlockSpec(memory_space=pltpu.VMEM)],
        out_specs=pl.BlockSpec(memory_space=pltpu.VMEM),
        scratch_shapes=[
            pltpu.VMEM((8, 32, 2048), BF16),
            pltpu.VMEM((4, 1024, 256), BF16),
            pltpu.VMEM((4, 1024, 256), BF16),
            pltpu.VMEM((8, 2, 256, 1), F32),
            pltpu.VMEM((8, 2, 256, 1), F32),
            pltpu.VMEM((8, 2, 256, 128), F32),
            pltpu.VMEM((8, 2, 32, 128), F32),
            pltpu.VMEM((8, 2, 256, 128), F32),
            pltpu.VMEM((8, 2, 32, 128), F32),
            pltpu.SemaphoreType.DMA((8,)),
            pltpu.SemaphoreType.DMA((8,)),
            pltpu.SemaphoreType.DMA((2,)),
            pltpu.SemaphoreType.DMA((6,)),
            pltpu.SemaphoreType.DMA((6,)),
            pltpu.SemaphoreType.DMA((2, 8)),
            pltpu.SemaphoreType.DMA((2, 8)),
        ],
        compiler_params=pltpu.CompilerParams(
            collective_id=0, has_side_effects=True, vmem_limit_bytes=48 * 1024 * 1024
        ),
        name="attend",
    )(q, k, v, loc)


class Ring:
    def __init__(self, piece, ssem, rsem, base, dev, me):
        self.piece, self.ssem, self.rsem, self.base, self.dev = piece, ssem, rsem, base, dev
        self.plus, self.minus, self.opp = around(me, 1), around(me, 3), around(me, 2)
        self.up = [self.copy(me, h, h, self.plus) for h in range(2)]
        self.down = [self.copy(me, h, 2 + h, self.minus) for h in range(2)]
        self.on_up = self.copy(self.minus, 0, 4, self.plus)
        self.on_down = self.copy(self.plus, 1, 5, self.minus)

    def copy(self, origin, half, n, peer):
        ref = self.piece(origin, half)
        return remote(ref, ref, self.ssem.at[self.base + n], self.rsem.at[self.base + n], self.dev(peer))

    def start(self):
        self.up[0].start()
        self.down[1].start()
        self.up[1].start()
        self.down[0].start()

    def forward(self):
        self.up[0].wait_recv()
        self.on_up.start()
        self.down[1].wait_recv()
        self.on_down.start()

    def near(self):
        self.up[1].wait_recv()
        self.down[0].wait_recv()

    def far(self):
        self.on_up.wait_recv()
        self.on_down.wait_recv()

    def sent(self):
        for c in (*self.up, *self.down, self.on_up, self.on_down):
            c.wait_send()


def run_rings(rings):
    for r in rings:
        r.start()
    for r in rings:
        r.forward()
    for r in rings:
        r.near()
    for r in rings:
        r.far()


class Swap:
    def __init__(self, buf, ssem, rsem, base, dev, me):
        self.copies = [
            remote(buf.at[me], buf.at[me], ssem.at[base + d], rsem.at[base + d], dev(around(me, d)))
            for d in (1, 2, 3)
        ]

    def run(self):
        for c in self.copies:
            c.start()
        for c in self.copies:
            c.wait_recv()

    def sent(self):
        for c in self.copies:
            c.wait_send()


def finish_kernel(
    attn_ref, proj_hbm, skip_ref, gain_ref, lex_hbm, div_ref, tok_ref,
    hidden_ref, logprob_ref,
    rows_all, proj, mixed, from_core, from_y, sq, sq_y, norm, lex, stat, stat_c,
    l_s, s_s, r_s,
):
    z, x, yh = lax.axis_index("ctx_0"), lax.axis_index("ctx_1"), lax.axis_index("ctx_2")
    yl, core = lax.axis_index("head_0"), lax.axis_index("head_1")
    y = 2 * yh + yl
    other = 1 - core

    lex_copy = pltpu.make_async_copy(lex_hbm, lex, l_s.at[0])
    proj_copy = pltpu.make_async_copy(proj_hbm, proj, l_s.at[1])
    proj_copy.start()
    lex_copy.start()

    for d in (1, 2, 3):
        greet(at_z(around(z, d)))
        greet(at_x(around(x, d)))
        greet(at_y(around(y, d)))
    greet(at_core(other))
    pl.semaphore_wait(pltpu.get_barrier_semaphore(), 10)

    pending = []
    count = [0]

    def take(n):
        count[0] += n
        return count[0] - n

    def ring(piece, dev, me):
        r = Ring(piece, s_s, r_s, take(6), dev, me)
        pending.append(r.sent)
        return r

    def single(src, dst, dev):
        n = take(1)
        c = remote(src, dst, s_s.at[n], r_s.at[n], dev)
        pending.append(c.wait_send)
        return c

    def swap(buf, dev, me):
        s = Swap(buf, s_s, r_s, take(4), dev, me)
        pending.append(s.sent)
        s.run()

    rows_all[x, z, yh] = attn_ref[...]
    pair = single(rows_all.at[x, z, yh], rows_all.at[x, z, yh], {"ctx_2": 1 - yh})
    pair.start()
    pair.wait_recv()

    def half_cols(h):
        return pl.ds(h * 1024, 1024)

    lo, hi = pl.ds(0, 16), pl.ds(16, 16)
    run_rings([
        ring(lambda o, h: rows_all.at[x, o, :, lo, half_cols(h)], at_z, z),
        ring(lambda o, h: rows_all.at[o, z, :, hi, half_cols(h)], at_x, x),
    ])
    run_rings([
        ring(lambda o, h: rows_all.at[o, :, :, lo, half_cols(h)], at_x, x),
        ring(lambda o, h: rows_all.at[:, o, :, hi, half_cols(h)], at_z, z),
    ])

    proj_copy.wait()
    w = proj[...]
    for q in range(4):
        a = rows_all[q].reshape(256, 2048)
        mixed[q // 2, q % 2] = jnp.dot(a, w, preferred_element_type=F32)
    c = single(mixed.at[:, other], from_core, at_core(other))
    c.start()
    c.wait_recv()
    mine = mixed.at[:, core]
    for q in range(2):
        from_core[q] = mine[q] + from_core[q]
    c = single(from_core.at[1 - yl], from_y, {"head_0": 1 - yl})
    c.start()
    c.wait_recv()
    hidden = (skip_ref[...].astype(F32) + (from_core[yl] + from_y[...])).astype(BF16)
    hidden_ref[...] = hidden
    wide = hidden.astype(F32)

    part = jnp.sum(jnp.transpose(wide * wide), axis=0, keepdims=True)
    for stage, (dev, me) in enumerate(((at_z, z), (at_x, x))):
        sq[stage, me] = jnp.broadcast_to(part, (8, 256))
        swap(sq.at[stage], dev, me)
        part = sq[stage, 0, 0:1] + sq[stage, 1, 0:1] + sq[stage, 2, 0:1] + sq[stage, 3, 0:1]
    sq_y[yh] = jnp.broadcast_to(part, (8, 256))
    c = single(sq_y.at[yh], sq_y.at[yh], {"ctx_2": 1 - yh})
    c.start()
    c.wait_recv()
    part = sq_y[0, 0:1] + sq_y[1, 0:1]
    factor = jnp.transpose(jnp.broadcast_to(lax.rsqrt(part / D + EPS), (256, 256)))
    norm[z, x, y, core] = (wide * factor * gain_ref[...]).astype(BF16)

    r0, r1, r2 = pl.ds(0, 96), pl.ds(96, 80), pl.ds(176, 80)

    def cols(h):
        return pl.ds(h * 128, 128)

    run_rings([
        ring(lambda o, h: norm.at[o, x, y, core, r0, cols(h)], at_z, z),
        ring(lambda o, h: norm.at[z, o, y, core, r1, cols(h)], at_x, x),
        ring(lambda o, h: norm.at[z, x, o, core, r2, cols(h)], at_y, y),
    ])
    run_rings([
        ring(lambda o, h: norm.at[:, o, y, core, r0, cols(h)], at_x, x),
        ring(lambda o, h: norm.at[z, :, o, core, r1, cols(h)], at_y, y),
        ring(lambda o, h: norm.at[o, x, :, core, r2, cols(h)], at_z, z),
    ])
    last = [
        ring(lambda o, h: norm.at[:, :, o, core, r0, cols(h)], at_y, y),
        ring(lambda o, h: norm.at[o, :, :, core, r1, cols(h)], at_z, z),
        ring(lambda o, h: norm.at[:, o, :, core, r2, cols(h)], at_x, x),
    ]
    parts = [
        lambda o: norm.at[:, :, o, core, r0],
        lambda o: norm.at[o, :, :, core, r1],
        lambda o: norm.at[:, o, :, core, r2],
    ]
    arrivals = []

    def hand_over(ref):
        c = single(ref, ref, at_core(other))
        c.start()
        arrivals.append(c)

    for r in last:
        r.start()
    for f, own in zip(parts, (y, z, x)):
        hand_over(f(own))
    for r in last:
        r.forward()
    for r, f in zip(last, parts):
        r.near()
        hand_over(f(r.plus))
        hand_over(f(r.minus))
    for r, f in zip(last, parts):
        r.far()
        hand_over(f(r.opp))
    for c in arrivals:
        c.wait_recv()
    lex_copy.wait()

    offset = (((z * 4 + x) * 2 + yh) * 4 + yl * 2 + core) * 512
    for group in range(4):
        def add(zz, total):
            a = jnp.concatenate(
                [norm[zz, i // 2, 2 * (i % 2) + group // 2, group % 2] for i in range(8)], axis=1
            )
            first = pl.multiple_of(zz * 2048, 2048)
            return total + jnp.dot(a, lex[pl.ds(first, 2048), :], preferred_element_type=F32)

        rows = slice(group * 256, (group + 1) * 256)
        logits = lax.fori_loop(0, 4, add, jnp.zeros((256, 512), F32)) / div_ref[rows, :]
        ids = lax.broadcasted_iota(jnp.int32, logits.shape, 1) + offset
        picked = jnp.sum(jnp.where(ids == tok_ref[rows, :], logits, 0.0), axis=1, keepdims=True)
        peak = jnp.max(logits, axis=1, keepdims=True)
        total = jnp.sum(jnp.exp(logits - peak), axis=1, keepdims=True)
        lane = lax.broadcasted_iota(jnp.int32, (256, 128), 1)
        both = jnp.where(lane == 0, peak, jnp.where(lane == 1, total, picked))
        stat[0, z, :, rows] = jnp.transpose(both)[0:8, :]

    def joined(tiles):
        peak = tiles[0][0:1]
        for t in tiles[1:]:
            peak = jnp.maximum(peak, t[0:1])
        total = sum(t[1:2] * jnp.exp(t[0:1] - peak) for t in tiles)
        picked = sum(t[2:3] for t in tiles)
        return peak, total, picked

    def spread(values):
        sub = lax.broadcasted_iota(jnp.int32, (8, 1024), 0)
        return jnp.where(sub == 0, values[0], jnp.where(sub == 1, values[1], values[2]))

    values = None
    for stage, (dev, me) in enumerate(((at_z, z), (at_x, x), (at_y, y))):
        if stage:
            stat[stage, me] = spread(values)
        swap(stat.at[stage], dev, me)
        values = joined([stat[stage, i] for i in range(4)])
    stat_c[core] = spread(values)
    c = single(stat_c.at[core], stat_c.at[core], at_core(other))
    c.start()
    c.wait_recv()
    peak, total, picked = joined([stat_c[0], stat_c[1]])
    logprob_ref[...] = picked - peak - jnp.log(total)

    for wait in pending:
        wait()


def finish(attn, proj, skip, gain, lex, div, tok):
    vmem = pl.BlockSpec(memory_space=pltpu.VMEM)
    hbm = pl.BlockSpec(memory_space=pl.ANY)
    return pl.pallas_call(
        finish_kernel,
        out_shape=(
            jax.ShapeDtypeStruct((256, 256), BF16),
            jax.ShapeDtypeStruct((1, 1024), F32),
        ),
        in_specs=[vmem, hbm, vmem, vmem, hbm, vmem, vmem],
        out_specs=(vmem, vmem),
        scratch_shapes=[
            pltpu.VMEM((4, 4, 2, 32, 2048), BF16),
            pltpu.VMEM((2048, 256), BF16),
            pltpu.VMEM((2, 2, 256, 256), F32),
            pltpu.VMEM((2, 256, 256), F32),
            pltpu.VMEM((256, 256), F32),
            pltpu.VMEM((2, 4, 8, 256), F32),
            pltpu.VMEM((2, 8, 256), F32),
            pltpu.VMEM((4, 4, 4, 2, 256, 256), BF16),
            pltpu.VMEM((8192, 512), BF16),
            pltpu.VMEM((3, 4, 8, 1024), F32),
            pltpu.VMEM((2, 8, 1024), F32),
            pltpu.SemaphoreType.DMA((2,)),
            pltpu.SemaphoreType.DMA((128,)),
            pltpu.SemaphoreType.DMA((128,)),
        ],
        compiler_params=pltpu.CompilerParams(
            collective_id=1, has_side_effects=True, vmem_limit_bytes=56 * 1024 * 1024
        ),
        name="finish",
    )(attn, proj, skip, gain, lex, div, tok)


def shards(q, k, v, loc, proj, skip, gain, lex, div, tok):
    attn = attend(q, k, v, loc.reshape(1024, 1))
    hidden, logprob = finish(
        attn, proj, skip, gain.reshape(1, 256), lex, div.reshape(1024, 1), tok.reshape(1024, 1)
    )
    return hidden, logprob.reshape(1024)


def solution(mesh):
    torus = Mesh(mesh.devices.reshape(4, 4, 2, 2, 2), CTX_HEAD)
    placed = (
        P(CTX, HEAD),
        P(CTX, HEAD),
        P(CTX, HEAD),
        P(),
        P(HEAD, CTX),
        P(HEAD, CTX),
        P(CTX),
        P(None, CTX_HEAD),
        P(),
        P(),
    )
    return jax.shard_map(
        shards, mesh=torus, in_specs=placed, out_specs=(P(HEAD, CTX), P()), check_vma=False
    )
```

time: 1000 us -> 237 us (0.24)
  waiting for transfers between devices: 765 us -> 0 us
  Pallas kernels: 0 us -> 225 us
  matrix products: 101 us -> 0 us
  blocking collectives: 66.2 us -> 0 us
  other arithmetic: 28.6 us -> 0 us
  between operations: 14.1 us -> 0.67 us
    all_gather x4 -> x0, waiting for transfers between devices: 398 us -> none  [the longest x1 154 us: shards(): lax.all_gather(full_rows, HEAD, axis=0, tiled=True)]
    reduce_scatter x1 -> x0, waiting for transfers between devices: 357 us -> none  [sent_together(): result = lax.psum_scatter(both, axis, scatter_dimension=dim, tiled=True)]
    pallas_call x0 -> x2, Pallas kernels: none -> 225 us  [the longest x1 135 us: finish(): pl.pallas_call(finish_kernel, out_shape=(jax.ShapeDtypeStruct((256, 256),...]
    dot_general x10 -> x0, matrix products: 101 us -> none  [the longest x4 46.7 us: local_attention(): jnp.einsum('qhd,kd->qhk', query_heads[row_start:row_start + row_block, kv...]
    all_gather x5 -> x0, blocking collectives: 34.9 us -> none  [collected_together(): both, at, found = (lax.all_gather(jnp.concatenate(lines), axis), 0, {})]
    all_to_all x2 -> x0, blocking collectives: 31.3 us -> none  [the longest x1 16.9 us: sent_and_summed(): tiles = lax.all_to_all(in_blocks(x, dim, devices), axis, 0, 0, tiled=True)]
    reduce_sum x5 -> x0, other arithmetic: 11.8 us -> none  [the longest x1 11.1 us: local_attention(): head_sum.append(jnp.sum(weights, axis=-1))]
  transfers between devices with their start and end apart: 6 -> 0, of which waited for: 6 -> 0; matrix products, arithmetic and copies ran while one was open for 1% -> 0% of each run, Pallas kernels for 0% -> 0%
where the time goes in v1:
time: 237 us; the launch traced here: 236 us
  Pallas kernels  225 us (95%)
  local copies, waits for them, and re-layouts  10.8 us (5%)
    pallas_call x1, Pallas kernels, finish(): pl.pallas_call(finish_kernel, out_shape=(jax.ShapeDtypeStruct((256, 256),...  135 us
    pallas_call x1, Pallas kernels, attend(): pl.pallas_call(attend_kernel, out_shape=jax.ShapeDtypeStruct((32, 2048),...  90.1 us
    unnamed x10, local copies, waits for them, and re-layouts  6.47 us

profile of v1, /device:TPU:1, one launch (start us, length us, event | category | flops | bytes accessed | tf_op | source)
XLA Modules:
  0.0 236.1 jit_solution(14591786350931026902)
XLA Ops:
  0.6 0.9 copy.12.loc_ref
  1.5 0.0 copy-start.1
  1.6 1.0 copy-done.1
  2.6 0.0 copy-start.2
  2.6 1.0 copy-done.2
  3.6 0.0 copy-start.3
  3.6 0.9 copy-done.3
  4.5 90.1 %attend.1.attn_ref = bf16[32,2048]{1,0:T(8,128)(2,1)S(1)} custom-call(bf16[32,2048]{1,0:T(8,128)(2,1)S(1)} %copy-done.3, bf16[1024,256]{1,0:T(8,128)(2,1)S(1)} %copy-done.1, bf16[1024,256]{1,0:T(8,128)(2,1)S(1)} %copy-done.2, s32[1024,1]{1,0:T(8,128)S(1)} %copy.12.loc_ref), custom_call_target="tpu_custom_call" | custom-call | tf_op jit(solution)/shard_map/attend/pallas_call | solution.py:240
  94.7 0.0 copy-start
  94.7 0.6 copy-done
  95.3 1.7 copy.13.div_ref
  97.0 1.7 copy.14.tok_ref
  98.7 134.6 %finish.1 = (bf16[256,256]{1,0:T(8,128)(2,1)}, f32[1,1024]{1,0:T(1,128)}) custom-call(bf16[32,2048]{1,0:T(8,128)(2,1)} %copy-done, bf16[2048,256]{1,0:T(8,128)(2,1)} %proj_hbm.1, bf16[256,256]{1,0:T(8,128)(2,1)} %skip_ref.1, f32[1,256]{1,0:T(1,128)} %bitcast.9, bf16[8192,512]{1,0:T(8,128)(2,1)} %lex_hbm.1, f32[1024,1]{1,0:T(8,128)} %copy.13.div_ref, ...), custom_call_target="tpu_custom_call" | custom-call | tf_op jit(solution)/shard_map/finish/pallas_call | solution.py:532
  233.3 1.6 copy.17
  234.9 1.3 copy.18
Async XLA Ops:
  1.5 1.0 copy-start.1
  2.6 1.0 copy-start.2
  3.6 0.9 copy-start.3
  94.7 0.7 copy-start

commit v2 on v1

v2 whole, which is shorter than its diff:
```python
import jax
import jax.numpy as jnp
from jax import lax
from jax.experimental import pallas as pl
from jax.experimental.pallas import tpu as pltpu
from jax.sharding import Mesh
from jax.sharding import PartitionSpec as P

D = 8192
EPS = 1e-05
LOW = -1e30
LOG2E = 1.4426950408889634
EXP2_SCALE = 128 ** (-0.5) * LOG2E
CTX = ("ctx_0", "ctx_1", "ctx_2")
HEAD = ("head_0", "head_1")
CTX_HEAD = CTX + HEAD
F32 = jnp.float32
BF16 = jnp.bfloat16
MESH = pl.DeviceIdType.MESH


def at_z(p):
    return {"ctx_0": p}


def at_x(p):
    return {"ctx_1": p}


def at_y(p):
    return {"ctx_2": lax.div(p, 2), "head_0": lax.rem(p, 2)}


def at_core(p):
    return {"head_1": p}


def around(p, d):
    return lax.rem(p + d, 4)


def remote(src, dst, ssem, rsem, dev):
    return pltpu.make_async_remote_copy(
        src_ref=src, dst_ref=dst, send_sem=ssem, recv_sem=rsem, device_id=dev, device_id_type=MESH
    )


def greet(dev):
    pl.semaphore_signal(pltpu.get_barrier_semaphore(), inc=1, device_id=dev, device_id_type=MESH)


class Ring:
    def __init__(self, piece, ssem, rsem, base, dev, me):
        self.piece, self.ssem, self.rsem, self.base, self.dev = piece, ssem, rsem, base, dev
        self.plus, self.minus, self.opp = around(me, 1), around(me, 3), around(me, 2)
        self.up = [self.copy(me, h, h, self.plus) for h in range(2)]
        self.down = [self.copy(me, h, 2 + h, self.minus) for h in range(2)]
        self.on_up = self.copy(self.minus, 0, 4, self.plus)
        self.on_down = self.copy(self.plus, 1, 5, self.minus)

    def copy(self, origin, half, n, peer):
        ref = self.piece(origin, half)
        return remote(ref, ref, self.ssem.at[self.base + n], self.rsem.at[self.base + n], self.dev(peer))

    def start(self):
        self.up[0].start()
        self.down[1].start()
        self.up[1].start()
        self.down[0].start()

    def forward(self):
        self.up[0].wait_recv()
        self.on_up.start()
        self.down[1].wait_recv()
        self.on_down.start()

    def near(self):
        self.up[1].wait_recv()
        self.down[0].wait_recv()

    def far(self):
        self.on_up.wait_recv()
        self.on_down.wait_recv()

    def sent(self):
        for c in (*self.up, *self.down, self.on_up, self.on_down):
            c.wait_send()


def run_rings(rings):
    for r in rings:
        r.start()
    for r in rings:
        r.forward()
    for r in rings:
        r.near()
    for r in rings:
        r.far()


class Swap:
    def __init__(self, buf, ssem, rsem, base, dev, me):
        self.copies = [
            remote(buf.at[me], buf.at[me], ssem.at[base + d], rsem.at[base + d], dev(around(me, d)))
            for d in (1, 2, 3)
        ]

    def run(self):
        for c in self.copies:
            c.start()
        for c in self.copies:
            c.wait_recv()

    def sent(self):
        for c in self.copies:
            c.wait_send()


def column(row):
    return jnp.transpose(jnp.broadcast_to(row, (128, row.shape[1])))[:, 0:1]


def kernel(
    q_hbm, k_hbm, v_hbm, loc_ref, proj_hbm, skip_ref, gain_ref, lex_hbm, div_ref, tok_ref,
    hidden_ref, logprob_ref,
    qbuf, kbuf, vbuf, loc_col, m_s, l_s, acc, part_stat, racc, rstat,
    rows_all, proj, mixed, from_core, from_y, sq, sq_y, norm, lex, stat, stat_c,
    l_sem, s_s, r_s,
):
    z, x, yh = lax.axis_index("ctx_0"), lax.axis_index("ctx_1"), lax.axis_index("ctx_2")
    yl, core = lax.axis_index("head_0"), lax.axis_index("head_1")
    y = 2 * yh + yl
    other, mate = 1 - core, 1 - yh
    diagonal = x == z

    proj_copy = pltpu.make_async_copy(proj_hbm, proj, l_sem.at[0])
    lex_copy = pltpu.make_async_copy(lex_hbm, lex, l_sem.at[1])

    def head_cols(ref, g):
        return ref.at[:, pl.ds(pl.multiple_of(g * 128, 128), 128)]

    own_k = pltpu.make_async_copy(head_cols(k_hbm, yh), kbuf.at[z, yh], l_sem.at[2])
    own_v = pltpu.make_async_copy(head_cols(v_hbm, yh), vbuf.at[z, yh], l_sem.at[3])
    own_k.start()
    own_v.start()

    for d in (1, 2, 3):
        greet(at_z(around(z, d)))
        greet(at_x(around(x, d)))
        greet(at_y(around(y, d)))
    greet(at_core(other))
    for i in range(2):
        @pl.when(jnp.logical_not(diagonal & (i == yh)))
        def _():
            greet({"ctx_0": x, "ctx_1": z, "ctx_2": i})
    pl.semaphore_wait(pltpu.get_barrier_semaphore(), 10 + jnp.where(diagonal, 1, 2))

    pending = []
    count = [0]

    def take(n):
        count[0] += n
        return count[0] - n

    def ring(piece, dev, me):
        r = Ring(piece, s_s, r_s, take(6), dev, me)
        pending.append(r.sent)
        return r

    def single(src, dst, dev):
        n = take(1)
        c = remote(src, dst, s_s.at[n], r_s.at[n], dev)
        pending.append(c.wait_send)
        return c

    def swap(buf, dev, me):
        s = Swap(buf, s_s, r_s, take(4), dev, me)
        pending.append(s.sent)
        s.run()

    q_at = take(2)

    def q_copies(i):
        src = q_hbm.at[:, i * 1024 : (i + 1) * 1024]
        dst = qbuf.at[z, pl.ds(pl.multiple_of(yh * 32, 32), 32)]
        return src, dst

    def q_send(i):
        peer = {"ctx_0": x, "ctx_1": z, "ctx_2": i}
        return remote(*q_copies(i), s_s.at[q_at + i], r_s.at[q_at + yh], peer)

    for i in range(2):
        to_self = diagonal & (i == yh)
        @pl.when(jnp.logical_not(to_self))
        def _():
            q_send(i).start()
        @pl.when(to_self)
        def _():
            pltpu.make_async_copy(*q_copies(i), r_s.at[q_at + yh]).start()

    k_swap = single(head_cols(k_hbm, mate), kbuf.at[z, yh], {"ctx_2": mate})
    v_swap = single(head_cols(v_hbm, mate), vbuf.at[z, yh], {"ctx_2": mate})
    k_swap.start()
    v_swap.start()

    def kv_ring(yo):
        return ring(lambda o, h: (vbuf if h else kbuf).at[o, yo], at_z, z)

    own_ring, mate_ring = kv_ring(yh), kv_ring(mate)
    own_k.wait()
    own_v.wait()
    own_ring.start()

    m_s[...] = jnp.full(m_s.shape, LOW, F32)
    l_s[...] = jnp.zeros(l_s.shape, F32)
    acc[...] = jnp.zeros(acc.shape, F32)
    for i in range(8):
        cols = slice(i * 128, (i + 1) * 128)
        loc_col[cols, :] = jnp.transpose(jnp.broadcast_to(loc_ref[:, cols], (128, 128)))

    for i in range(2):
        dst = qbuf.at[x, i * 32 : (i + 1) * 32]
        remote(dst, dst, s_s.at[q_at], r_s.at[q_at + i], at_x(around(x, 1))).wait_recv()
    q_ring = ring(lambda o, h: qbuf.at[o, :, h * 512 : (h + 1) * 512], at_x, x)
    q_ring.start()
    k_swap.wait_recv()
    v_swap.wait_recv()
    mate_ring.start()
    q_ring.forward()
    proj_copy.start()
    q_ring.near()
    q_ring.far()

    def tile(s, c, zo, yo, masked):
        q = jnp.concatenate(
            [qbuf[s, c * 32 : (c + 1) * 32, j * 128 : (j + 1) * 128] for j in range(8)], axis=0
        )
        raw = lax.dot_general(
            q, kbuf[zo, yo], (((1,), (1,)), ((), ())), preferred_element_type=F32
        )
        if masked:
            base = 8 * zo + 2 * x + yo
            first = pl.multiple_of(base * 32, 32)
            loc = loc_col[pl.ds(first, 32), 0:1] - base * 1024
            loc = jnp.concatenate([loc] * 8, axis=0)
            pos = lax.broadcasted_iota(jnp.int32, raw.shape, 1)
            raw = jnp.where(pos <= loc, raw, LOW)
        top = jnp.max(raw, axis=1, keepdims=True)
        w = jnp.exp2((raw - top) * EXP2_SCALE)
        total = jnp.sum(w, axis=1, keepdims=True)
        part = jnp.dot(w.astype(BF16), vbuf[zo, yo], preferred_element_type=F32)
        m_old = m_s[s, c]
        m_new = jnp.maximum(m_old, top)
        a = jnp.exp2((m_old - m_new) * EXP2_SCALE)
        b = jnp.exp2((top - m_new) * EXP2_SCALE)
        m_s[s, c] = m_new
        l_s[s, c] = l_s[s, c] * a + total * b
        acc[s, c] = acc[s, c] * a + part * b

    def work(s, zo, yo):
        chunk = 8 * s + 2 * z
        block = 8 * zo + 2 * x + yo

        @pl.when(chunk > block)
        def _():
            tile(s, 0, zo, yo, False)
            tile(s, 1, zo, yo, False)

        @pl.when(chunk == block)
        def _():
            tile(s, 0, zo, yo, True)
            tile(s, 1, zo, yo, False)

        @pl.when(chunk + 1 == block)
        def _():
            tile(s, 1, zo, yo, True)

    part_at = take(8)

    def acc_copy(s):
        return remote(acc.at[s], racc.at[x], s_s.at[part_at + s], r_s.at[part_at + x], at_x(s))

    def stat_copy(s):
        return remote(part_stat.at[s], rstat.at[x], s_s.at[part_at + 4 + s],
                      r_s.at[part_at + 4 + x], at_x(s))

    @pl.loop(0, 8)
    def _(p):
        @pl.when(p == 2)
        def _():
            own_ring.forward()
            own_ring.up[1].wait_recv()

        @pl.when(p == 3)
        def _():
            own_ring.down[0].wait_recv()

        @pl.when(p == 4)
        def _():
            mate_ring.forward()
            mate_ring.up[1].wait_recv()

        @pl.when(p == 5)
        def _():
            mate_ring.down[0].wait_recv()

        @pl.when(p == 6)
        def _():
            own_ring.far()

        @pl.when(p == 7)
        def _():
            mate_ring.far()

        step = jnp.where(p < 2, 0, jnp.where(p >= 6, 2, jnp.where(lax.rem(p, 2) == 0, 3, 1)))
        is_own = (p == 0) | (p == 2) | (p == 3) | (p == 6)
        zo = around(z, step)
        yo = jnp.where(is_own, yh, mate)

        @pl.loop(0, 4)
        def _(i):
            s = around(x, jnp.where(i == 0, 2, jnp.where(i == 1, 1, jnp.where(i == 2, 3, 0))))
            work(s, zo, yo)

            @pl.when(p == 7)
            def _():
                lane = lax.broadcasted_iota(jnp.int32, (32, 128), 1)
                for c in range(2):
                    t = jnp.zeros((32, 128), F32)
                    for j in range(8):
                        rows = slice(j * 32, (j + 1) * 32)
                        t = jnp.where(lane == j, m_s[s, c, rows, :], t)
                        t = jnp.where(lane == 8 + j, l_s[s, c, rows, :], t)
                    part_stat[s, c] = t

                @pl.when(s != x)
                def _():
                    acc_copy(s).start()
                    stat_copy(s).start()

                @pl.when(s == x)
                def _():
                    pltpu.make_async_copy(acc.at[s], racc.at[x], r_s.at[part_at + x]).start()
                    pltpu.make_async_copy(part_stat.at[s], rstat.at[x], r_s.at[part_at + 4 + x]).start()

    lex_copy.start()
    for i in range(4):
        remote(part_stat.at[i], rstat.at[i], s_s.at[part_at + 4 + i], r_s.at[part_at + 4 + i],
               at_x(around(x, 1))).wait_recv()
        remote(acc.at[i], racc.at[i], s_s.at[part_at + i], r_s.at[part_at + i],
               at_x(around(x, 1))).wait_recv()

    for c in range(2):
        tops = [rstat[i, c] for i in range(4)]
        sums = [pltpu.roll(t, 120, 1) for t in tops]
        top = jnp.maximum(jnp.maximum(tops[0], tops[1]), jnp.maximum(tops[2], tops[3]))
        shares = [jnp.exp2((t - top) * EXP2_SCALE) for t in tops]
        den = sum(a * b for a, b in zip(shares, sums))
        joined_rows = []
        for j in range(8):
            rows = slice(j * 32, (j + 1) * 32)
            num = sum(shares[i][:, j : j + 1] * racc[i, c, rows, :] for i in range(4))
            joined_rows.append((num / den[:, j : j + 1]).astype(BF16))
        rows_all[x, z, c * 32 : (c + 1) * 32, pl.ds(pl.multiple_of(yh * 1024, 1024), 1024)] = (
            jnp.concatenate(joined_rows, axis=1)
        )
    for i in range(4):
        @pl.when(i != x)
        def _():
            acc_copy(i).wait_send()
            stat_copy(i).wait_send()
    for i in range(2):
        @pl.when(jnp.logical_not(diagonal & (i == yh)))
        def _():
            q_send(i).wait_send()

    own_cols = pl.ds(pl.multiple_of(yh * 1024, 1024), 1024)
    pair = single(rows_all.at[x, z, :, own_cols], rows_all.at[x, z, :, own_cols], {"ctx_2": mate})
    pair.start()
    pair.wait_recv()

    def half_cols(h):
        return pl.ds(h * 1024, 1024)

    lo, hi = pl.ds(0, 32), pl.ds(32, 32)
    run_rings([
        ring(lambda o, h: rows_all.at[x, o, lo, half_cols(h)], at_z, z),
        ring(lambda o, h: rows_all.at[o, z, hi, half_cols(h)], at_x, x),
    ])
    run_rings([
        ring(lambda o, h: rows_all.at[o, :, lo, half_cols(h)], at_x, x),
        ring(lambda o, h: rows_all.at[:, o, hi, half_cols(h)], at_z, z),
    ])

    proj_copy.wait()
    w = proj[...]
    for q in range(4):
        a = rows_all[q].reshape(256, 2048)
        mixed[q // 2, q % 2] = jnp.dot(a, w, preferred_element_type=F32)
    c = single(mixed.at[:, other], from_core, at_core(other))
    c.start()
    c.wait_recv()
    mine = mixed.at[:, core]
    for q in range(2):
        from_core[q] = mine[q] + from_core[q]
    c = single(from_core.at[1 - yl], from_y, {"head_0": 1 - yl})
    c.start()
    c.wait_recv()
    hidden = (skip_ref[...].astype(F32) + (from_core[yl] + from_y[...])).astype(BF16)
    hidden_ref[...] = hidden
    wide = hidden.astype(F32)

    part = jnp.sum(jnp.transpose(wide * wide), axis=0, keepdims=True)
    for stage, (dev, me) in enumerate(((at_z, z), (at_x, x))):
        sq[stage, me] = jnp.broadcast_to(part, (8, 256))
        swap(sq.at[stage], dev, me)
        part = sq[stage, 0, 0:1] + sq[stage, 1, 0:1] + sq[stage, 2, 0:1] + sq[stage, 3, 0:1]
    sq_y[yh] = jnp.broadcast_to(part, (8, 256))
    c = single(sq_y.at[yh], sq_y.at[yh], {"ctx_2": 1 - yh})
    c.start()
    c.wait_recv()
    part = sq_y[0, 0:1] + sq_y[1, 0:1]
    factor = jnp.transpose(jnp.broadcast_to(lax.rsqrt(part / D + EPS), (256, 256)))
    norm[z, x, y, core] = (wide * factor * gain_ref[...]).astype(BF16)

    r0, r1, r2 = pl.ds(0, 96), pl.ds(96, 80), pl.ds(176, 80)

    def cols(h):
        return pl.ds(h * 128, 128)

    run_rings([
        ring(lambda o, h: norm.at[o, x, y, core, r0, cols(h)], at_z, z),
        ring(lambda o, h: norm.at[z, o, y, core, r1, cols(h)], at_x, x),
        ring(lambda o, h: norm.at[z, x, o, core, r2, cols(h)], at_y, y),
    ])
    run_rings([
        ring(lambda o, h: norm.at[:, o, y, core, r0, cols(h)], at_x, x),
        ring(lambda o, h: norm.at[z, :, o, core, r1, cols(h)], at_y, y),
        ring(lambda o, h: norm.at[o, x, :, core, r2, cols(h)], at_z, z),
    ])
    last = [
        ring(lambda o, h: norm.at[:, :, o, core, r0, cols(h)], at_y, y),
        ring(lambda o, h: norm.at[o, :, :, core, r1, cols(h)], at_z, z),
        ring(lambda o, h: norm.at[:, o, :, core, r2, cols(h)], at_x, x),
    ]
    parts = [
        lambda o: norm.at[:, :, o, core, r0],
        lambda o: norm.at[o, :, :, core, r1],
        lambda o: norm.at[:, o, :, core, r2],
    ]
    arrivals = []

    def hand_over(ref):
        c = single(ref, ref, at_core(other))
        c.start()
        arrivals.append(c)

    for r in last:
        r.start()
    for f, own in zip(parts, (y, z, x)):
        hand_over(f(own))
    for r in last:
        r.forward()
    for r, f in zip(last, parts):
        r.near()
        hand_over(f(r.plus))
        hand_over(f(r.minus))
    for r, f in zip(last, parts):
        r.far()
        hand_over(f(r.opp))
    for c in arrivals:
        c.wait_recv()
    lex_copy.wait()

    offset = (((z * 4 + x) * 2 + yh) * 4 + yl * 2 + core) * 512
    for group in range(4):
        def add(zz, total):
            a = jnp.concatenate(
                [norm[zz, i // 2, 2 * (i % 2) + group // 2, group % 2] for i in range(8)], axis=1
            )
            first = pl.multiple_of(zz * 2048, 2048)
            return total + jnp.dot(a, lex[pl.ds(first, 2048), :], preferred_element_type=F32)

        rows = slice(group * 256, (group + 1) * 256)
        logits = lax.fori_loop(0, 4, add, jnp.zeros((256, 512), F32)) / column(div_ref[:, rows])
        ids = lax.broadcasted_iota(jnp.int32, logits.shape, 1) + offset
        picked = jnp.sum(jnp.where(ids == column(tok_ref[:, rows]), logits, 0.0), axis=1, keepdims=True)
        peak = jnp.max(logits, axis=1, keepdims=True)
        total = jnp.sum(jnp.exp(logits - peak), axis=1, keepdims=True)
        lane = lax.broadcasted_iota(jnp.int32, (256, 128), 1)
        both = jnp.where(lane == 0, peak, jnp.where(lane == 1, total, picked))
        stat[0, z, :, rows] = jnp.transpose(both)[0:8, :]

    def joined(tiles):
        peak = tiles[0][0:1]
        for t in tiles[1:]:
            peak = jnp.maximum(peak, t[0:1])
        total = sum(t[1:2] * jnp.exp(t[0:1] - peak) for t in tiles)
        picked = sum(t[2:3] for t in tiles)
        return peak, total, picked

    def spread(values):
        sub = lax.broadcasted_iota(jnp.int32, (8, 1024), 0)
        return jnp.where(sub == 0, values[0], jnp.where(sub == 1, values[1], values[2]))

    values = None
    for stage, (dev, me) in enumerate(((at_z, z), (at_x, x), (at_y, y))):
        if stage:
            stat[stage, me] = spread(values)
        swap(stat.at[stage], dev, me)
        values = joined([stat[stage, i] for i in range(4)])
    stat_c[core] = spread(values)
    c = single(stat_c.at[core], stat_c.at[core], at_core(other))
    c.start()
    c.wait_recv()
    peak, total, picked = joined([stat_c[0], stat_c[1]])
    logprob_ref[...] = picked - peak - jnp.log(total)

    for wait in pending:
        wait()


def whole(q, k, v, loc, proj, skip, gain, lex, div, tok):
    vmem = pl.BlockSpec(memory_space=pltpu.VMEM)
    hbm = pl.BlockSpec(memory_space=pl.ANY)
    return pl.pallas_call(
        kernel,
        out_shape=(
            jax.ShapeDtypeStruct((256, 256), BF16),
            jax.ShapeDtypeStruct((1, 1024), F32),
        ),
        in_specs=[hbm, hbm, hbm, vmem, hbm, vmem, vmem, hbm, vmem, vmem],
        out_specs=(vmem, vmem),
        scratch_shapes=[
            pltpu.VMEM((4, 64, 1024), BF16),
            pltpu.VMEM((4, 2, 1024, 128), BF16),
            pltpu.VMEM((4, 2, 1024, 128), BF16),
            pltpu.VMEM((1024, 128), jnp.int32),
            pltpu.VMEM((4, 2, 256, 1), F32),
            pltpu.VMEM((4, 2, 256, 1), F32),
            pltpu.VMEM((4, 2, 256, 128), F32),
            pltpu.VMEM((4, 2, 32, 128), F32),
            pltpu.VMEM((4, 2, 256, 128), F32),
            pltpu.VMEM((4, 2, 32, 128), F32),
            pltpu.VMEM((4, 4, 64, 2048), BF16),
            pltpu.VMEM((2048, 256), BF16),
            pltpu.VMEM((2, 2, 256, 256), F32),
            pltpu.VMEM((2, 256, 256), F32),
            pltpu.VMEM((256, 256), F32),
            pltpu.VMEM((2, 4, 8, 256), F32),
            pltpu.VMEM((2, 8, 256), F32),
            pltpu.VMEM((4, 4, 4, 2, 256, 256), BF16),
            pltpu.VMEM((8192, 512), BF16),
            pltpu.VMEM((3, 4, 8, 1024), F32),
            pltpu.VMEM((2, 8, 1024), F32),
            pltpu.SemaphoreType.DMA((4,)),
            pltpu.SemaphoreType.DMA((160,)),
            pltpu.SemaphoreType.DMA((160,)),
        ],
        compiler_params=pltpu.CompilerParams(
            collective_id=0, has_side_effects=True, vmem_limit_bytes=58 * 1024 * 1024
        ),
        name="whole",
    )(q, k, v, loc, proj, skip, gain, lex, div, tok)


def shards(q, k, v, loc, proj, skip, gain, lex, div, tok):
    hidden, logprob = whole(
        q, k, v, loc.reshape(1, 1024), proj, skip, gain.reshape(1, 256), lex,
        div.reshape(1, 1024), tok.reshape(1, 1024)
    )
    return hidden, logprob.reshape(1024)


def solution(mesh):
    torus = Mesh(mesh.devices.reshape(4, 4, 2, 2, 2), CTX_HEAD)
    placed = (
        P(CTX, HEAD),
        P(CTX, HEAD),
        P(CTX, HEAD),
        P(),
        P(HEAD, CTX),
        P(HEAD, CTX),
        P(CTX),
        P(None, CTX_HEAD),
        P(),
        P(),
    )
    return jax.shard_map(
        shards, mesh=torus, in_specs=placed, out_specs=(P(HEAD, CTX), P()), check_vma=False
    )
```

time: 237 us -> 202 us (0.85)
  Pallas kernels: 225 us -> 198 us
  local copies, waits for them, and re-layouts: 10.8 us -> 2.85 us
    pallas_call x2 -> x1, Pallas kernels: 225 us -> 198 us  [whole(): pl.pallas_call(kernel, out_shape=(jax.ShapeDtypeStruct((256, 256), BF16),...]
    reshape x3 -> x0, local copies, waits for them, and re-layouts: 4.32 us -> none  [the longest x1 1.71 us: shards(): div.reshape(1024, 1)]
    unnamed x10 -> x2, local copies, waits for them, and re-layouts: 6.47 us -> 2.85 us
where the time goes in v2:
time: 202 us; the launch traced here: 201 us
  Pallas kernels  198 us (98%)
  local copies, waits for them, and re-layouts  2.85 us (1%)
    pallas_call x1, Pallas kernels, whole(): pl.pallas_call(kernel, out_shape=(jax.ShapeDtypeStruct((256, 256), BF16),...  198 us

profile of v2, /device:TPU:1, one launch (start us, length us, event | category | flops | bytes accessed | tf_op | source)
XLA Modules:
  0.0 201.5 jit_solution(5893921153860496125)
XLA Ops:
  0.6 198.0 %whole.1 = (bf16[256,256]{1,0:T(8,128)(2,1)}, f32[1,1024]{1,0:T(1,128)}) custom-call(bf16[32,2048]{1,0:T(8,128)(2,1)} %q_hbm.1, bf16[1024,256]{1,0:T(8,128)(2,1)} %k_hbm.1, bf16[1024,256]{1,0:T(8,128)(2,1)} %v_hbm.1, s32[1,1024]{1,0:T(1,128)} %bitcast.5, bf16[2048,256]{1,0:T(8,128)(2,1)} %proj_hbm.1, bf16[256,256]{1,0:T(8,128)(2,1)} %skip_ref.1, ...), custom_call_target="tpu_custom_call" | custom-call | tf_op jit(solution)/shard_map/whole/pallas_call | solution.py:526
  198.6 1.6 copy.14
  200.2 1.3 copy.15

commit v3 on v2

--- a/solution.py
+++ b/solution.py
@@ -9,6 +9,7 @@
 D = 8192
 EPS = 1e-05
 LOW = -1e30
+GROUPS = 2
 LOG2E = 1.4426950408889634
 EXP2_SCALE = 128 ** (-0.5) * LOG2E
 CTX = ("ctx_0", "ctx_1", "ctx_2")
@@ -124,7 +125,7 @@
     q_hbm, k_hbm, v_hbm, loc_ref, proj_hbm, skip_ref, gain_ref, lex_hbm, div_ref, tok_ref,
     hidden_ref, logprob_ref,
     qbuf, kbuf, vbuf, loc_col, m_s, l_s, acc, part_stat, racc, rstat,
-    rows_all, proj, mixed, from_core, from_y, sq, sq_y, norm, lex, stat, stat_c,
+    rows_all, proj, mixed, from_core, from_y, skip, gain, back, sq_c, sq, norm, lex, logit, stat, stat_c,
     l_sem, s_s, r_s,
 ):
     z, x, yh = lax.axis_index("ctx_0"), lax.axis_index("ctx_1"), lax.axis_index("ctx_2")
@@ -132,8 +133,11 @@
     y = 2 * yh + yl
     other, mate = 1 - core, 1 - yh
     diagonal = x == z
-
-    proj_copy = pltpu.make_async_copy(proj_hbm, proj, l_sem.at[0])
+    head = 2 * yl + core
+    twin = {"ctx_1": head, "head_0": lax.div(x, 2), "head_1": lax.rem(x, 2)}
+    is_twin = x == head
+
+    proj_copy = pltpu.make_async_copy(proj_hbm, proj.at[x], l_sem.at[0])
     lex_copy = pltpu.make_async_copy(lex_hbm, lex, l_sem.at[1])
 
     def head_cols(ref, g):
@@ -143,17 +147,25 @@
     own_v = pltpu.make_async_copy(head_cols(v_hbm, yh), vbuf.at[z, yh], l_sem.at[3])
     own_k.start()
     own_v.start()
+    proj_copy.start()
 
     for d in (1, 2, 3):
         greet(at_z(around(z, d)))
         greet(at_x(around(x, d)))
         greet(at_y(around(y, d)))
+        for e in (1, 2, 3):
+            greet({**at_z(around(z, d)), **at_y(around(y, e))})
     greet(at_core(other))
     for i in range(2):
         @pl.when(jnp.logical_not(diagonal & (i == yh)))
         def _():
             greet({"ctx_0": x, "ctx_1": z, "ctx_2": i})
-    pl.semaphore_wait(pltpu.get_barrier_semaphore(), 10 + jnp.where(diagonal, 1, 2))
+    @pl.when(jnp.logical_not(is_twin))
+    def _():
+        greet(twin)
+    pl.semaphore_wait(
+        pltpu.get_barrier_semaphore(), 19 + jnp.where(diagonal, 1, 2) + jnp.where(is_twin, 0, 1)
+    )
 
     pending = []
     count = [0]
@@ -177,6 +189,22 @@
         s = Swap(buf, s_s, r_s, take(4), dev, me)
         pending.append(s.sent)
         s.run()
+
+    def to_twin(src, dst, n):
+        @pl.when(is_twin)
+        def _():
+            pltpu.make_async_copy(src, dst, r_s.at[n]).start()
+        @pl.when(jnp.logical_not(is_twin))
+        def _():
+            remote(src, dst, s_s.at[n], r_s.at[n], twin).start()
+
+    def from_twin(src, dst, n):
+        remote(src, dst, s_s.at[n], r_s.at[n], twin).wait_recv()
+
+    def twin_sent(src, dst, n):
+        @pl.when(jnp.logical_not(is_twin))
+        def _():
+            remote(src, dst, s_s.at[n], r_s.at[n], twin).wait_send()
 
     q_at = take(2)
 
@@ -223,13 +251,20 @@
         remote(dst, dst, s_s.at[q_at], r_s.at[q_at + i], at_x(around(x, 1))).wait_recv()
     q_ring = ring(lambda o, h: qbuf.at[o, :, h * 512 : (h + 1) * 512], at_x, x)
     q_ring.start()
+    own_ring.forward()
+    q_ring.forward()
+
+    proj_copy.wait()
+    proj_ring = ring(lambda o, h: proj.at[o, h * 1024 : (h + 1) * 1024], at_x, x)
+    proj_ring.start()
     k_swap.wait_recv()
     v_swap.wait_recv()
     mate_ring.start()
-    q_ring.forward()
-    proj_copy.start()
     q_ring.near()
     q_ring.far()
+    skip_at = take(2)
+    to_twin(skip_ref, skip, skip_at)
+    to_twin(gain_ref, gain, skip_at + 1)
 
     def tile(s, c, zo, yo, masked):
         q = jnp.concatenate(
@@ -288,21 +323,21 @@
     def _(p):
         @pl.when(p == 2)
         def _():
-            own_ring.forward()
             own_ring.up[1].wait_recv()
 
         @pl.when(p == 3)
         def _():
             own_ring.down[0].wait_recv()
+            mate_ring.forward()
 
         @pl.when(p == 4)
         def _():
-            mate_ring.forward()
             mate_ring.up[1].wait_recv()
 
         @pl.when(p == 5)
         def _():
             mate_ring.down[0].wait_recv()
+            proj_ring.forward()
 
         @pl.when(p == 6)
         def _():
@@ -361,7 +396,7 @@
             rows = slice(j * 32, (j + 1) * 32)
             num = sum(shares[i][:, j : j + 1] * racc[i, c, rows, :] for i in range(4))
             joined_rows.append((num / den[:, j : j + 1]).astype(BF16))
-        rows_all[x, z, c * 32 : (c + 1) * 32, pl.ds(pl.multiple_of(yh * 1024, 1024), 1024)] = (
+        rows_all[z, c * 32 : (c + 1) * 32, pl.ds(pl.multiple_of(yh * 1024, 1024), 1024)] = (
             jnp.concatenate(joined_rows, axis=1)
         )
     for i in range(4):
@@ -374,54 +409,71 @@
         def _():
             q_send(i).wait_send()
 
+    def rows_at(o, yo, h):
+        return rows_all.at[o, :, pl.ds(pl.multiple_of(yo * 1024 + h * 512, 512), 512)]
+
     own_cols = pl.ds(pl.multiple_of(yh * 1024, 1024), 1024)
-    pair = single(rows_all.at[x, z, :, own_cols], rows_all.at[x, z, :, own_cols], {"ctx_2": mate})
+    pair = single(rows_all.at[z, :, own_cols], rows_all.at[z, :, own_cols], {"ctx_2": mate})
     pair.start()
+    own_rows = ring(lambda o, h: rows_at(o, yh, h), at_z, z)
+    mate_rows = ring(lambda o, h: rows_at(o, mate, h), at_z, z)
+    own_rows.start()
     pair.wait_recv()
-
-    def half_cols(h):
-        return pl.ds(h * 1024, 1024)
-
-    lo, hi = pl.ds(0, 32), pl.ds(32, 32)
-    run_rings([
-        ring(lambda o, h: rows_all.at[x, o, lo, half_cols(h)], at_z, z),
-        ring(lambda o, h: rows_all.at[o, z, hi, half_cols(h)], at_x, x),
-    ])
-    run_rings([
-        ring(lambda o, h: rows_all.at[o, :, lo, half_cols(h)], at_x, x),
-        ring(lambda o, h: rows_all.at[:, o, hi, half_cols(h)], at_z, z),
-    ])
-
-    proj_copy.wait()
-    w = proj[...]
-    for q in range(4):
-        a = rows_all[q].reshape(256, 2048)
-        mixed[q // 2, q % 2] = jnp.dot(a, w, preferred_element_type=F32)
-    c = single(mixed.at[:, other], from_core, at_core(other))
+    mate_rows.start()
+    own_rows.forward()
+    mate_rows.forward()
+    for r in (own_rows, mate_rows):
+        r.near()
+        r.far()
+    proj_ring.near()
+    proj_ring.far()
+
+    def project(a, b):
+        return jnp.dot(
+            rows_all[...].reshape(256, 2048), proj[2 * a + b], preferred_element_type=F32
+        )
+
+    crossings = []
+    for q in range(2):
+        mixed[q, other] = project(q, other)
+        c = single(mixed.at[q, other], from_core.at[q], at_core(other))
+        c.start()
+        crossings.append(c)
+    for q in range(2):
+        mixed[q, core] = project(q, core)
+    for q, c in enumerate(crossings):
+        c.wait_recv()
+        from_core[q] = mixed[q, core] + from_core[q]
+    c = single(from_core.at[1 - yl], from_y, {"head_0": 1 - yl})
+    c.start()
+    from_twin(skip_ref, skip, skip_at)
+    from_twin(gain_ref, gain, skip_at + 1)
+    c.wait_recv()
+    hidden = (skip[...].astype(F32) + (from_core[yl] + from_y[...])).astype(BF16)
+    back[0] = hidden
+    back_at = take(1)
+    to_twin(back.at[0], back.at[1], back_at)
+    wide = hidden.astype(F32)
+
+    part = jnp.sum(jnp.transpose(wide * wide), axis=0, keepdims=True)
+    sq_c[core] = jnp.broadcast_to(part, (8, 256))
+    c = single(sq_c.at[core], sq_c.at[core], at_core(other))
     c.start()
     c.wait_recv()
-    mine = mixed.at[:, core]
-    for q in range(2):
-        from_core[q] = mine[q] + from_core[q]
-    c = single(from_core.at[1 - yl], from_y, {"head_0": 1 - yl})
-    c.start()
-    c.wait_recv()
-    hidden = (skip_ref[...].astype(F32) + (from_core[yl] + from_y[...])).astype(BF16)
-    hidden_ref[...] = hidden
-    wide = hidden.astype(F32)
-
-    part = jnp.sum(jnp.transpose(wide * wide), axis=0, keepdims=True)
-    for stage, (dev, me) in enumerate(((at_z, z), (at_x, x))):
-        sq[stage, me] = jnp.broadcast_to(part, (8, 256))
-        swap(sq.at[stage], dev, me)
-        part = sq[stage, 0, 0:1] + sq[stage, 1, 0:1] + sq[stage, 2, 0:1] + sq[stage, 3, 0:1]
-    sq_y[yh] = jnp.broadcast_to(part, (8, 256))
-    c = single(sq_y.at[yh], sq_y.at[yh], {"ctx_2": 1 - yh})
-    c.start()
-    c.wait_recv()
-    part = sq_y[0, 0:1] + sq_y[1, 0:1]
+    sq[z, y] = sq_c[0] + sq_c[1]
+    shared = []
+    for d in range(4):
+        for e in range(4):
+            if d or e:
+                peer = {**at_z(around(z, d)), **at_y(around(y, e))}
+                c = single(sq.at[z, y], sq.at[z, y], peer)
+                c.start()
+                shared.append(c)
+    for c in shared:
+        c.wait_recv()
+    part = sum(sq[i // 4, i % 4, 0:1] for i in range(16))
     factor = jnp.transpose(jnp.broadcast_to(lax.rsqrt(part / D + EPS), (256, 256)))
-    norm[z, x, y, core] = (wide * factor * gain_ref[...]).astype(BF16)
+    norm[z, x, y, core] = (wide * factor * gain[...]).astype(BF16)
 
     r0, r1, r2 = pl.ds(0, 96), pl.ds(96, 80), pl.ds(176, 80)
 
@@ -468,21 +520,35 @@
     for r, f in zip(last, parts):
         r.far()
         hand_over(f(r.opp))
+    lex_copy.wait()
+
+    def add(cc, fresh):
+        for zz in range(4):
+            first = zz * 2048 + cc * 512
+            b = jnp.concatenate(
+                [lex[pl.ds(pl.multiple_of(first + i * 1024, 512), 512), :] for i in range(2)], axis=0
+            )
+            for g in range(0, 4, GROUPS):
+                a = jnp.concatenate([
+                    jnp.concatenate([norm[zz, q, yy, cc] for yy in (0, 2, 1, 3)], axis=1)
+                    for q in range(g, g + GROUPS)
+                ], axis=0)
+                t = jnp.dot(a, b, preferred_element_type=F32)
+                rows = slice(g * 256, (g + GROUPS) * 256)
+                if fresh and zz == 0:
+                    logit[rows, :] = t
+                else:
+                    logit[rows, :] += t
+
+    add(core, True)
     for c in arrivals:
         c.wait_recv()
-    lex_copy.wait()
+    add(other, False)
 
     offset = (((z * 4 + x) * 2 + yh) * 4 + yl * 2 + core) * 512
     for group in range(4):
-        def add(zz, total):
-            a = jnp.concatenate(
-                [norm[zz, i // 2, 2 * (i % 2) + group // 2, group % 2] for i in range(8)], axis=1
-            )
-            first = pl.multiple_of(zz * 2048, 2048)
-            return total + jnp.dot(a, lex[pl.ds(first, 2048), :], preferred_element_type=F32)
-
         rows = slice(group * 256, (group + 1) * 256)
-        logits = lax.fori_loop(0, 4, add, jnp.zeros((256, 512), F32)) / column(div_ref[:, rows])
+        logits = logit[rows, :] / column(div_ref[:, rows])
         ids = lax.broadcasted_iota(jnp.int32, logits.shape, 1) + offset
         picked = jnp.sum(jnp.where(ids == column(tok_ref[:, rows]), logits, 0.0), axis=1, keepdims=True)
         peak = jnp.max(logits, axis=1, keepdims=True)
@@ -516,6 +582,11 @@
     peak, total, picked = joined([stat_c[0], stat_c[1]])
     logprob_ref[...] = picked - peak - jnp.log(total)
 
+    from_twin(back.at[0], back.at[1], back_at)
+    hidden_ref[...] = back[1]
+    twin_sent(skip_ref, skip, skip_at)
+    twin_sent(gain_ref, gain, skip_at + 1)
+    twin_sent(back.at[0], back.at[1], back_at)
     for wait in pending:
         wait()
 
@@ -542,20 +613,24 @@
             pltpu.VMEM((4, 2, 32, 128), F32),
             pltpu.VMEM((4, 2, 256, 128), F32),
             pltpu.VMEM((4, 2, 32, 128), F32),
-            pltpu.VMEM((4, 4, 64, 2048), BF16),
-            pltpu.VMEM((2048, 256), BF16),
+            pltpu.VMEM((4, 64, 2048), BF16),
+            pltpu.VMEM((4, 2048, 256), BF16),
             pltpu.VMEM((2, 2, 256, 256), F32),
             pltpu.VMEM((2, 256, 256), F32),
             pltpu.VMEM((256, 256), F32),
-            pltpu.VMEM((2, 4, 8, 256), F32),
+            pltpu.VMEM((256, 256), BF16),
+            pltpu.VMEM((1, 256), F32),
+            pltpu.VMEM((2, 256, 256), BF16),
             pltpu.VMEM((2, 8, 256), F32),
+            pltpu.VMEM((4, 4, 8, 256), F32),
             pltpu.VMEM((4, 4, 4, 2, 256, 256), BF16),
             pltpu.VMEM((8192, 512), BF16),
+            pltpu.VMEM((1024, 512), F32),
             pltpu.VMEM((3, 4, 8, 1024), F32),
             pltpu.VMEM((2, 8, 1024), F32),
             pltpu.SemaphoreType.DMA((4,)),
-            pltpu.SemaphoreType.DMA((160,)),
-            pltpu.SemaphoreType.DMA((160,)),
+            pltpu.SemaphoreType.DMA((192,)),
+            pltpu.SemaphoreType.DMA((192,)),
         ],
         compiler_params=pltpu.CompilerParams(
             collective_id=0, has_side_effects=True, vmem_limit_bytes=58 * 1024 * 1024

time: 202 us -> 181 us (0.90)
  Pallas kernels: 198 us -> 177 us
    pallas_call x1, Pallas kernels: 198 us -> 177 us  [whole(): pl.pallas_call(kernel, out_shape=(jax.ShapeDtypeStruct((256, 256), BF16),...]
where the time goes in v3:
time: 181 us; the launch traced here: 180 us
  Pallas kernels  177 us (98%)
  local copies, waits for them, and re-layouts  2.85 us (2%)
    pallas_call x1, Pallas kernels, whole(): pl.pallas_call(kernel, out_shape=(jax.ShapeDtypeStruct((256, 256), BF16),...  177 us

profile of v3, /device:TPU:1, one launch (start us, length us, event | category | flops | bytes accessed | tf_op | source)
XLA Modules:
  0.0 180.4 jit_solution(7462651513250918984)
XLA Ops:
  0.6 176.9 %whole.1 = (bf16[256,256]{1,0:T(8,128)(2,1)}, f32[1,1024]{1,0:T(1,128)}) custom-call(bf16[32,2048]{1,0:T(8,128)(2,1)} %q_hbm.1, bf16[1024,256]{1,0:T(8,128)(2,1)} %k_hbm.1, bf16[1024,256]{1,0:T(8,128)(2,1)} %v_hbm.1, s32[1,1024]{1,0:T(1,128)} %bitcast.5, bf16[2048,256]{1,0:T(8,128)(2,1)} %proj_hbm.1, bf16[256,256]{1,0:T(8,128)(2,1)} %skip_ref.1, ...), custom_call_target="tpu_custom_call" | custom-call | tf_op jit(solution)/shard_map/whole/pallas_call | solution.py:597
  177.5 1.6 copy.14
  179.1 1.3 copy.15

commit v4 on v3

--- a/solution.py
+++ b/solution.py
@@ -122,8 +122,9 @@
 
 
 def kernel(
-    q_hbm, k_hbm, v_hbm, loc_ref, proj_hbm, skip_ref, gain_ref, lex_hbm, div_ref, tok_ref,
+    q_hbm, k_hbm, v_hbm, loc_hbm, proj_hbm, skip_ref, gain_ref, lex_hbm, div_hbm, tok_hbm,
     hidden_ref, logprob_ref,
+    loc_ref, div_ref, tok_ref,
     qbuf, kbuf, vbuf, loc_col, m_s, l_s, acc, part_stat, racc, rstat,
     rows_all, proj, mixed, from_core, from_y, skip, gain, back, sq_c, sq, norm, lex, logit, stat, stat_c,
     l_sem, s_s, r_s,
@@ -145,9 +146,15 @@
 
     own_k = pltpu.make_async_copy(head_cols(k_hbm, yh), kbuf.at[z, yh], l_sem.at[2])
     own_v = pltpu.make_async_copy(head_cols(v_hbm, yh), vbuf.at[z, yh], l_sem.at[3])
+    small = [
+        pltpu.make_async_copy(a, b, l_sem.at[4 + i])
+        for i, (a, b) in enumerate(((loc_hbm, loc_ref), (div_hbm, div_ref), (tok_hbm, tok_ref)))
+    ]
     own_k.start()
     own_v.start()
     proj_copy.start()
+    for c in small:
+        c.start()
 
     for d in (1, 2, 3):
         greet(at_z(around(z, d)))
@@ -242,6 +249,8 @@
     m_s[...] = jnp.full(m_s.shape, LOW, F32)
     l_s[...] = jnp.zeros(l_s.shape, F32)
     acc[...] = jnp.zeros(acc.shape, F32)
+    for c in small:
+        c.wait()
     for i in range(8):
         cols = slice(i * 128, (i + 1) * 128)
         loc_col[cols, :] = jnp.transpose(jnp.broadcast_to(loc_ref[:, cols], (128, 128)))
@@ -257,11 +266,13 @@
     proj_copy.wait()
     proj_ring = ring(lambda o, h: proj.at[o, h * 1024 : (h + 1) * 1024], at_x, x)
     proj_ring.start()
+
     k_swap.wait_recv()
     v_swap.wait_recv()
     mate_ring.start()
     q_ring.near()
     q_ring.far()
+
     skip_at = take(2)
     to_twin(skip_ref, skip, skip_at)
     to_twin(gain_ref, gain, skip_at + 1)
@@ -433,19 +444,28 @@
             rows_all[...].reshape(256, 2048), proj[2 * a + b], preferred_element_type=F32
         )
 
-    crossings = []
-    for q in range(2):
-        mixed[q, other] = project(q, other)
-        c = single(mixed.at[q, other], from_core.at[q], at_core(other))
-        c.start()
-        crossings.append(c)
-    for q in range(2):
-        mixed[q, core] = project(q, core)
-    for q, c in enumerate(crossings):
-        c.wait_recv()
-        from_core[q] = mixed[q, core] + from_core[q]
-    c = single(from_core.at[1 - yl], from_y, {"head_0": 1 - yl})
+    cross_at = take(2)
+    away = 1 - yl
+    mixed[away, other] = project(away, other)
+    crossing_away = remote(
+        mixed.at[away, other], from_core.at[away], s_s.at[cross_at], r_s.at[cross_at + away], at_core(other)
+    )
+    crossing_away.start()
+    mixed[away, core] = project(away, core)
+    mixed[yl, other] = project(yl, other)
+    crossing_home = remote(
+        mixed.at[yl, other], from_core.at[yl], s_s.at[cross_at + 1], r_s.at[cross_at + yl], at_core(other)
+    )
+    crossing_home.start()
+    crossing_away.wait_recv()
+    from_core[away] = mixed[away, core] + from_core[away]
+    c = single(from_core.at[away], from_y, {"head_0": away})
     c.start()
+    mixed[yl, core] = project(yl, core)
+    crossing_home.wait_recv()
+    from_core[yl] = mixed[yl, core] + from_core[yl]
+    pending.append(crossing_away.wait_send)
+    pending.append(crossing_home.wait_send)
     from_twin(skip_ref, skip, skip_at)
     from_twin(gain_ref, gain, skip_at + 1)
     c.wait_recv()
@@ -480,16 +500,22 @@
     def cols(h):
         return pl.ds(h * 128, 128)
 
-    run_rings([
-        ring(lambda o, h: norm.at[o, x, y, core, r0, cols(h)], at_z, z),
-        ring(lambda o, h: norm.at[z, o, y, core, r1, cols(h)], at_x, x),
-        ring(lambda o, h: norm.at[z, x, o, core, r2, cols(h)], at_y, y),
-    ])
+    own = norm.at[z, x, y, core]
+    near = []
+    for d in (2, 1, 3):
+        for rows, dev, me in ((r0, at_z, z), (r1, at_x, x), (r2, at_y, y)):
+            c = single(own.at[rows], own.at[rows], dev(around(me, d)))
+            c.start()
+            near.append(c)
+    for c in near:
+        c.wait_recv()
     run_rings([
         ring(lambda o, h: norm.at[:, o, y, core, r0, cols(h)], at_x, x),
         ring(lambda o, h: norm.at[z, :, o, core, r1, cols(h)], at_y, y),
         ring(lambda o, h: norm.at[o, x, :, core, r2, cols(h)], at_z, z),
     ])
+    earlier = list(pending)
+    pending.clear()
     last = [
         ring(lambda o, h: norm.at[:, :, o, core, r0, cols(h)], at_y, y),
         ring(lambda o, h: norm.at[o, :, :, core, r1, cols(h)], at_z, z),
@@ -513,6 +539,10 @@
         hand_over(f(own))
     for r in last:
         r.forward()
+    for wait in earlier:
+        wait()
+    twin_sent(skip_ref, skip, skip_at)
+    twin_sent(gain_ref, gain, skip_at + 1)
     for r, f in zip(last, parts):
         r.near()
         hand_over(f(r.plus))
@@ -584,8 +614,6 @@
 
     from_twin(back.at[0], back.at[1], back_at)
     hidden_ref[...] = back[1]
-    twin_sent(skip_ref, skip, skip_at)
-    twin_sent(gain_ref, gain, skip_at + 1)
     twin_sent(back.at[0], back.at[1], back_at)
     for wait in pending:
         wait()
@@ -600,9 +628,12 @@
             jax.ShapeDtypeStruct((256, 256), BF16),
             jax.ShapeDtypeStruct((1, 1024), F32),
         ),
-        in_specs=[hbm, hbm, hbm, vmem, hbm, vmem, vmem, hbm, vmem, vmem],
+        in_specs=[hbm] * 10,
         out_specs=(vmem, vmem),
         scratch_shapes=[
+            pltpu.VMEM((1, 1024), jnp.int32),
+            pltpu.VMEM((1, 1024), F32),
+            pltpu.VMEM((1, 1024), jnp.int32),
             pltpu.VMEM((4, 64, 1024), BF16),
             pltpu.VMEM((4, 2, 1024, 128), BF16),
             pltpu.VMEM((4, 2, 1024, 128), BF16),
@@ -628,7 +659,7 @@
             pltpu.VMEM((1024, 512), F32),
             pltpu.VMEM((3, 4, 8, 1024), F32),
             pltpu.VMEM((2, 8, 1024), F32),
-            pltpu.SemaphoreType.DMA((4,)),
+            pltpu.SemaphoreType.DMA((7,)),
             pltpu.SemaphoreType.DMA((192,)),
             pltpu.SemaphoreType.DMA((192,)),
         ],

time: 181 us -> 177 us (0.978)
  Pallas kernels: 177 us -> 173 us
    pallas_call x1, Pallas kernels: 177 us -> 173 us  [whole(): pl.pallas_call(kernel, out_shape=(jax.ShapeDtypeStruct((256, 256), BF16),...]
where the time goes in v4:
time: 177 us
  Pallas kernels  173 us (98%)
  local copies, waits for them, and re-layouts  2.85 us (2%)
    pallas_call x1, Pallas kernels, whole(): pl.pallas_call(kernel, out_shape=(jax.ShapeDtypeStruct((256, 256), BF16),...  173 us

profile of v4, /device:TPU:1, one launch (start us, length us, event | category | flops | bytes accessed | tf_op | source)
XLA Modules:
  0.0 176.7 jit_solution(5301698555497848235)
XLA Ops:
  0.6 173.3 %whole.1 = (bf16[256,256]{1,0:T(8,128)(2,1)}, f32[1,1024]{1,0:T(1,128)}) custom-call(bf16[32,2048]{1,0:T(8,128)(2,1)} %q_hbm.1, bf16[1024,256]{1,0:T(8,128)(2,1)} %k_hbm.1, bf16[1024,256]{1,0:T(8,128)(2,1)} %v_hbm.1, s32[1,1024]{1,0:T(1,128)} %bitcast.5, bf16[2048,256]{1,0:T(8,128)(2,1)} %proj_hbm.1, bf16[256,256]{1,0:T(8,128)(2,1)} %skip_ref.1, ...), custom_call_target="tpu_custom_call" | custom-call | tf_op jit(solution)/shard_map/whole/pallas_call | solution.py:625
  173.9 1.6 copy.14
  175.5 1.3 copy.15

commit v5 on v4

--- a/solution.py
+++ b/solution.py
@@ -344,11 +344,11 @@
         @pl.when(p == 4)
         def _():
             mate_ring.up[1].wait_recv()
+            proj_ring.forward()
 
         @pl.when(p == 5)
         def _():
             mate_ring.down[0].wait_recv()
-            proj_ring.forward()
 
         @pl.when(p == 6)
         def _():

time: 177 us -> 176 us (level)
  no operation moved by 1% of the time
where the time goes in v5:
time: 176 us; the launch traced here: 175 us
  Pallas kernels  172 us (98%)
  local copies, waits for them, and re-layouts  2.85 us (2%)
    pallas_call x1, Pallas kernels, whole(): pl.pallas_call(kernel, out_shape=(jax.ShapeDtypeStruct((256, 256), BF16),...  172 us

profile of v5, /device:TPU:1, one launch (start us, length us, event | category | flops | bytes accessed | tf_op | source)
XLA Modules:
  0.0 175.3 jit_solution(11987484749879040664)
XLA Ops:
  0.6 171.8 %whole.1 = (bf16[256,256]{1,0:T(8,128)(2,1)}, f32[1,1024]{1,0:T(1,128)}) custom-call(bf16[32,2048]{1,0:T(8,128)(2,1)} %q_hbm.1, bf16[1024,256]{1,0:T(8,128)(2,1)} %k_hbm.1, bf16[1024,256]{1,0:T(8,128)(2,1)} %v_hbm.1, s32[1,1024]{1,0:T(1,128)} %bitcast.5, bf16[2048,256]{1,0:T(8,128)(2,1)} %proj_hbm.1, bf16[256,256]{1,0:T(8,128)(2,1)} %skip_ref.1, ...), custom_call_target="tpu_custom_call" | custom-call | tf_op jit(solution)/shard_map/whole/pallas_call | solution.py:625
  172.5 1.6 copy.14
  174.1 1.3 copy.15
